TPU v7x, 32 devices: a whole 2x2x4 slice. The times are simulated.
32 devices in a mesh: gx: 8 (over y, x, core), gy: 4 (over z).
Axes of the slice: x: 2, y: 2, z: 4, core: 2. Of those that a mesh axis runs over, the one named last changes fastest.
Arguments:
- state_field: bfloat16 [192, 64, 1024], P(None, 'gy', 'gx'), may hold values from -6 to 6
- cotangent: bfloat16 [192, 64, 1024], P(None, 'gy', 'gx'), may hold values from -6 to 6
- ocean_mask: int32 [64, 1024], P('gy', 'gx'), may hold values from 0 to 1, as said below
- kernel: float32 [192, 7, 7], replicated, may hold values from -0.875 to 0.875
- inward_weight: bfloat16 [192, 768], replicated, may hold values from -0.4375 to 0.4375
- inward_bias: float32 [768], replicated, may hold values from -3 to 3
- outward_weight: bfloat16 [768, 192], replicated, may hold values from -0.21875 to 0.21875
- layer_scale: float32 [192], replicated, may hold values from 0.1 to 1.9
Outputs:
- output_field: bfloat16 [192, 64, 1024], P(None, 'gy', 'gx')
- field_grad: bfloat16 [192, 64, 1024], P(None, 'gy', 'gx')
- kernel_grad: float32 [192, 7, 7], replicated
- inward_grad: float32 [192, 768], replicated
- outward_grad: float32 [768, 192], replicated
Inputs may be any that keep to these rules, and one draw needn't show every extreme that they name: `ocean_mask`: land comes as whole blocks of 4 latitude rows by the 128 columns of one device, and as single cells.
All inputs are finite; a program needn't handle non-finite values.
Results may differ from a plain program's by a relative error of at most 0.0064.
Values may be sent and summed in bfloat16 or wider, within the bound.
A program may use at most 64 MiB of HBM per device.

v0:
```python
import math

import jax
import jax.numpy as jnp
from jax import lax
from jax.sharding import PartitionSpec as P


def padded_2(block, sides, width, periodic):
    for axis, dim in sides:
        count = lax.axis_size(axis)
        forward = [(i, i + 1) for i in range(count - 1)]
        if periodic:
            forward.append((count - 1, 0))
        backward = [(target, source) for source, target in forward]
        low = lax.ppermute(
            lax.slice_in_dim(block, block.shape[dim] - width, None, axis=dim), axis, forward
        )
        high = lax.ppermute(lax.slice_in_dim(block, 0, width, axis=dim), axis, backward)
        block = jnp.concatenate([low, block, high], axis=dim)
    return block


def from_partner(block, axis, distance):
    count = lax.axis_size(axis)
    route = []
    for low in range(count):
        high = low | 1 << distance
        if high != low and high < count:
            route += [(low, high), (high, low)]
    return lax.ppermute(block, axis, route)


def gelu_value(values):
    return 0.5 * values * (1.0 + jax.scipy.special.erf(values / math.sqrt(2.0)))


def gelu_slope(values):
    return 0.5 * (1.0 + jax.scipy.special.erf(values / math.sqrt(2.0))) + values * jnp.exp(
        -0.5 * values * values
    ) / math.sqrt(2.0 * math.pi)


def extend(source):
    lat_cells = source.shape[1]
    wrapped = padded_2(source, (("gx", 2),), 3, True)
    extended = padded_2(wrapped, (("gy", 1),), 3, False)
    top_strip = wrapped[:, lat_cells - 3 :, :]
    bit_total = lax.axis_size("gx").bit_length() - 1
    facing = top_strip
    for bit_number in range(bit_total):
        facing = from_partner(facing, "gx", bit_number)
    folded = jnp.flip(facing, (1, 2))
    at_top = lax.axis_index("gy") == lax.axis_size("gy") - 1
    upper_rows = jnp.where(at_top, folded, extended[:, lat_cells + 3 :, :])
    return jnp.concatenate([extended[:, : lat_cells + 3, :], upper_rows], axis=1)


def depthwise(padded, kernel, flipped):
    lat_cells = padded.shape[1] - 6
    lon_cells = padded.shape[2] - 6
    summed = jnp.zeros((padded.shape[0], lat_cells, lon_cells), jnp.float32)
    for row_tap in range(7):
        for col_tap in range(7):
            if flipped:
                weights = kernel[:, 6 - row_tap, 6 - col_tap]
            else:
                weights = kernel[:, row_tap, col_tap]
            window = padded[:, row_tap : row_tap + lat_cells, col_tap : col_tap + lon_cells].astype(
                jnp.float32
            )
            summed = summed + weights[:, None, None] * window
    return summed


def kernel_terms(grad_half, padded):
    lat_cells = grad_half.shape[1]
    lon_cells = grad_half.shape[2]
    grad_float = grad_half.astype(jnp.float32)
    row_sums = []
    for row_tap in range(7):
        column_sums = []
        for col_tap in range(7):
            window = padded[:, row_tap : row_tap + lat_cells, col_tap : col_tap + lon_cells].astype(
                jnp.float32
            )
            column_sums.append(jnp.sum(grad_float * window, axis=(1, 2)))
        row_sums.append(jnp.stack(column_sums, axis=1))
    return jnp.stack(row_sums, axis=1)


def mlp_block(
    conv_out, field_blk, cot_blk, mask_blk, inward_weight, inward_bias, outward_weight, layer_scale
):
    average = jnp.mean(conv_out, axis=0, keepdims=True)
    centered = conv_out - average
    variance = jnp.mean(centered * centered, axis=0, keepdims=True)
    inverse = lax.rsqrt(variance + 1e-06)
    normed = centered * inverse
    normed_half = normed.astype(jnp.bfloat16)
    contract = (((0,), (0,)), ((), ()))
    pre_act = (
        lax.dot_general(inward_weight, normed_half, contract, preferred_element_type=jnp.float32)
        + inward_bias[:, None]
    )
    hidden = gelu_value(pre_act).astype(jnp.bfloat16)
    branch = lax.dot_general(outward_weight, hidden, contract, preferred_element_type=jnp.float32)
    output_blk = (
        mask_blk * (field_blk.astype(jnp.float32) + layer_scale[:, None] * branch)
    ).astype(jnp.bfloat16)
    masked_grad = mask_blk * cot_blk.astype(jnp.float32)
    branch_grad = (layer_scale[:, None] * masked_grad).astype(jnp.bfloat16)
    rows_contract = (((1,), (1,)), ((), ()))
    outward_part = lax.dot_general(
        hidden, branch_grad, rows_contract, preferred_element_type=jnp.float32
    )
    hidden_grad = jnp.dot(outward_weight, branch_grad, preferred_element_type=jnp.float32)
    pre_grad = (hidden_grad * gelu_slope(pre_act)).astype(jnp.bfloat16)
    inward_part = lax.dot_general(
        normed_half, pre_grad, rows_contract, preferred_element_type=jnp.float32
    )
    normed_grad = jnp.dot(inward_weight, pre_grad, preferred_element_type=jnp.float32)
    mean_grad = jnp.mean(normed_grad, axis=0, keepdims=True)
    mean_prod = jnp.mean(normed_grad * normed, axis=0, keepdims=True)
    conv_grad = (inverse * (normed_grad - mean_grad - normed * mean_prod)).astype(jnp.bfloat16)
    return (output_blk, conv_grad, inward_part, outward_part)


def per_device(
    state_field,
    cotangent,
    ocean_mask,
    kernel,
    inward_weight,
    inward_bias,
    outward_weight,
    layer_scale,
):
    channels, lat_cells, lon_cells = state_field.shape
    hidden_units = inward_weight.shape[1]
    factor = 1.0 / math.sqrt(lat_cells * lon_cells)
    padded = extend(state_field)
    conv_out = depthwise(padded, kernel, False)
    block_cells = 4 * lon_cells
    block_count = lat_cells // 4
    flat_conv = conv_out.reshape(channels, lat_cells * lon_cells)
    flat_field = state_field.reshape(channels, lat_cells * lon_cells)
    flat_cot = cotangent.reshape(channels, lat_cells * lon_cells)
    mask_float = ocean_mask.astype(jnp.float32)
    flat_mask = mask_float.reshape(1, lat_cells * lon_cells)

    def block_step(block_index, state_tuple):
        out_flat, grad_flat, acc_in, acc_out = state_tuple
        offset = block_index * block_cells
        conv_blk = lax.dynamic_slice_in_dim(flat_conv, offset, block_cells, 1)
        field_blk = lax.dynamic_slice_in_dim(flat_field, offset, block_cells, 1)
        cot_blk = lax.dynamic_slice_in_dim(flat_cot, offset, block_cells, 1)
        mask_blk = lax.dynamic_slice_in_dim(flat_mask, offset, block_cells, 1)

        def compute_block(unused):
            return mlp_block(
                conv_blk,
                field_blk,
                cot_blk,
                mask_blk,
                inward_weight,
                inward_bias,
                outward_weight,
                layer_scale,
            )

        def skip_block(unused):
            zero_half = jnp.zeros((channels, block_cells), jnp.bfloat16)
            return (
                zero_half,
                zero_half,
                jnp.zeros((channels, hidden_units), jnp.float32),
                jnp.zeros((hidden_units, channels), jnp.float32),
            )

        output_blk, conv_grad, inward_part, outward_part = lax.cond(
            jnp.max(mask_blk) > 0.0, compute_block, skip_block, None
        )
        out_flat = lax.dynamic_update_slice_in_dim(out_flat, output_blk, offset, 1)
        grad_flat = lax.dynamic_update_slice_in_dim(grad_flat, conv_grad, offset, 1)
        return (out_flat, grad_flat, acc_in + inward_part, acc_out + outward_part)

    start_state = (
        jnp.zeros((channels, lat_cells * lon_cells), jnp.bfloat16),
        jnp.zeros((channels, lat_cells * lon_cells), jnp.bfloat16),
        jnp.zeros((channels, hidden_units), jnp.float32),
        jnp.zeros((hidden_units, channels), jnp.float32),
    )
    out_flat, grad_flat, acc_in, acc_out = lax.fori_loop(0, block_count, block_step, start_state)
    output_field = out_flat.reshape(channels, lat_cells, lon_cells)
    conv_grad = grad_flat.reshape(channels, lat_cells, lon_cells)
    grad_padded = extend(conv_grad)
    masked_grad = mask_float[None, :, :] * cotangent.astype(jnp.float32)
    field_grad = (masked_grad + depthwise(grad_padded, kernel, True)).astype(jnp.bfloat16)
    kernel_local = kernel_terms(conv_grad, padded) * factor
    inward_grad, outward_grad, kernel_grad = lax.psum(
        (acc_in * factor, acc_out * factor, kernel_local), ("gx", "gy")
    )
    return (output_field, field_grad, kernel_grad, inward_grad, outward_grad)


def solution(mesh):
    in_specs = (P(None, "gy", "gx"), P(None, "gy", "gx"), P("gy", "gx"), P(), P(), P(), P(), P())
    out_specs = (P(None, "gy", "gx"), P(None, "gy", "gx"), P(), P(), P())
    return jax.shard_map(
        per_device, mesh=mesh, in_specs=in_specs, out_specs=out_specs, check_vma=False
    )
```

profile of v0, /device:TPU:0, one launch (start us, length us, event | category | flops | bytes accessed | tf_op | source)
XLA Modules:
  0.0 334.0 jit_solution(14415250712640171347)
XLA Ops:
  11.0 2.9 collective-permute-start.1
  23.9 4.4 %collective-permute-done.4 = bf16[192,3,134]{0,2,1:T(8,128)(2,1)S(1)} collective-permute-done((bf16[192,3,134]{0,2,1:T(8,128)(2,1)S(1)}, bf16[192,3,134]{0,2,1:T(8,128)(2,1)S(1)}, u32[]{:S(2)}, u32[]{:S(2)}) %collective-permute-start.4) | collective-permute-done | bytes 154400 | tf_op jit(solution)/shard_map/ppermute | solution.py:31
  28.3 2.3 collective-permute-start.5
  31.2 3.7 %collective-permute-start.2 = (bf16[192,3,134]{0,2,1:T(8,128)(2,1)S(1)}, bf16[192,3,134]{0,2,1:T(8,128)(2,1)S(1)}, u32[]{:S(2)}, u32[]{:S(2)}) collective-permute-start(bf16[192,3,134]{0,2,1:T(8,128)(2,1)S(1)} %get-tuple-element.484), channel_id=1, source_target_pairs={{0,1},{1,2},{2,3},{4,5},{5,6},{6,7},{8,9},{9,10},{10,11},{12,13},{... | collective-permute-start | bytes 463112 | tf_op jit(solution)/shard_map/ppermute | solution.py:16
  38.2 2.3 maximum_maximum_fusion
  41.0 17.5 %fusion.74 = f32[192,16,128]{0,2,1:T(8,128)} fusion(bf16[192,16,128]{0,2,1:T(8,128)(2,1)S(1)} %copy-done.5, bf16[192,16,3]{0,2,1:T(4,128)(2,1)S(1)} %copy.18, bf16[192,16,3]{0,2,1:T(4,128)(2,1)S(1)} %copy.16, f32[192]{0:T(256)} %bitcast.54, f32[192]{0:T(256)} %bitcast.53, f32[192]{0:T(256)S(1)} %bitcast.276, f32[192]{0:T(256)S(1)} %bitcast.278, ...), kind=kLoop, calls=%fused_computation.191 | loop fusion | flops 64487424 | bytes 35463936 | tf_op jit(solution)/shard_map/add | solution.py:72
  58.5 2.8 copy.24
  63.2 72.3 %while.20 = (s32[]{:T(128)}, bf16[192,2048]{1,0:T(8,128)(2,1)}, bf16[192,2048]{1,0:T(8,128)(2,1)}, f32[192,768]{1,0:T(8,128)}, f32[768,192]{0,1:T(8,128)}, /*ind...) while((s32[]{:T(128)}, bf16[192,2048]{1,0:T(8,128)(2,1)}, ...), condition=%wide.region_8.9_spmd.clone, body=%wide.region_0.8_spmd.clone.sunk | while | flops 916292608 | bytes 30540056 | solution.py:194
  64.6 3.1 conditional.3
  75.0 3.1 conditional.3
  79.9 2.1 select_add_fusion.4
  85.5 18.3 %conditional.3 = (bf16[192,512]{1,0:T(8,128)(2,1)}, bf16[192,512]{1,0:T(8,128)(2,1)}, f32[192,768]{1,0:T(8,128)}, f32[768,192]{0,1:T(8,128)}) conditional(s32[]{:T(128)} %convert_element_type.1303, () %tuple.165, (f32[1,512]{1,0:T(1,128)S(1)}, bf16[192,2048]{1,0:T(8,128)(2,1)}, s32[]{:T(128)}, f32[192]{0:T(256)S(1)}, f32[192,2048]{1,0:T(8,128)}, ...), branch_computations={%region_2.2_spmd, %region_3.7_spmd} | conditional | flops 915702272 | bytes 21491112 | solution.py:181
  92.1 2.2 fusion.17
  97.2 2.4 fusion.20
  105.6 2.1 select_add_fusion.4
  111.2 18.3 %conditional.3 = (bf16[192,512]{1,0:T(8,128)(2,1)}, bf16[192,512]{1,0:T(8,128)(2,1)}, f32[192,768]{1,0:T(8,128)}, f32[768,192]{0,1:T(8,128)}) conditional(s32[]{:T(128)} %convert_element_type.1303, () %tuple.165, (f32[1,512]{1,0:T(1,128)S(1)}, bf16[192,2048]{1,0:T(8,128)(2,1)}, s32[]{:T(128)}, f32[192]{0:T(256)S(1)}, f32[192,2048]{1,0:T(8,128)}, ...), branch_computations={%region_2.2_spmd, %region_3.7_spmd} | conditional | flops 915702272 | bytes 21491112 | solution.py:181
  117.8 2.2 fusion.17
  123.0 2.4 fusion.20
  131.4 2.1 select_add_fusion.4
  135.6 2.2 copy.27
  137.8 7.4 %fusion.148 = (f32[192]{0:T(256)S(1)}, f32[192]{0:T(256)S(1)}, f32[192]{0:T(256)S(1)}, f32[192]{0:T(256)S(1)}, f32[192]{0:T(256)S(1)}, /*index=5*/f32[192]{0:T(2...) fusion(bf16[192,19,134]{0,2,1:T(8,128)(2,1)S(1)} %get-tuple-ele, ...), kind=kLoop, calls=%fused_computation.265 | loop fusion | flops 21623424 | bytes 14956032 | tf_op jit(solution)/shard_map/reduce_sum | solution.py:87
  145.2 2.1 fusion.130
  147.4 3.0 fusion.127
  150.4 6.6 %fusion.120 = (f32[192]{0:T(256)S(1)}, f32[192]{0:T(256)S(1)}, f32[192]{0:T(256)S(1)}, f32[192]{0:T(256)S(1)}, f32[192]{0:T(256)S(1)}, /*index=5*/f32[192]{0:T(2...) fusion(bf16[192,19,134]{0,2,1:T(8,128)(2,1)S(1)} %get-tuple-ele, ...), kind=kLoop, calls=%fused_computation.237 | loop fusion | flops 21623424 | bytes 14956032 | tf_op jit(solution)/shard_map/reduce_sum | solution.py:87
  158.9 13.4 %collective-permute-start.7 = (bf16[192,16,3]{0,1,2:T(8,128)(2,1)S(1)}, bf16[192,16,3]{0,1,2:T(8,128)(2,1)S(1)}, u32[]{:S(2)}, u32[]{:S(2)}) collective-permute-start(bf16[192,16,3]{0,1,2:T(8,128)(2,1)S(1)} %copy.28), channel_id=1, source_target_pairs={{0,4},{4,8},{8,12},{12,16},{16,20},{20,24},{24,28},{28,0},{1,5},{5... | collective-permute-start | bytes 55304 | tf_op jit(solution)/shard_map/ppermute | solution.py:16
  176.9 15.5 %collective-permute-start.11 = (bf16[192,3,134]{0,2,1:T(8,128)(2,1)S(1)}, bf16[192,3,134]{0,2,1:T(8,128)(2,1)S(1)}, u32[]{:S(2)}, u32[]{:S(2)}) collective-permute-start(bf16[192,3,134]{0,2,1:T(8,128)(2,1)S(1)} %collective-permute-done.10), channel_id=1, source_target_pairs={{0,8},{8,0},{4,12},{12,4},{16,24},{24,16},{20,28},{28,20},{1,9},{9... | collective-permute-start | bytes 463112 | tf_op jit(solution)/shard_map/ppermute | solution.py:31
  193.7 4.5 %collective-permute-done.11 = bf16[192,3,134]{0,2,1:T(8,128)(2,1)S(1)} collective-permute-done((bf16[192,3,134]{0,2,1:T(8,128)(2,1)S(1)}, bf16[192,3,134]{0,2,1:T(8,128)(2,1)S(1)}, u32[]{:S(2)}, u32[]{:S(2)}) %collective-permute-start.11) | collective-permute-done | bytes 154400 | tf_op jit(solution)/shard_map/ppermute | solution.py:31
  200.1 46.7 %psum.21 = f32[192,7,7]{0,2,1:T(8,128)} all-reduce(f32[192,7,7]{0,2,1:T(8,128)S(1)} %broadcast_multiply_fusion.5), channel_id=1, replica_groups=mesh['gx'=8,'gy'=4] {'gx','gy'}, use_global_device_ids=true, to_apply=%region_58.59 | all-reduce | flops 9408 | bytes 75264 | tf_op jit(solution)/shard_map/psum | solution.py:201
  246.8 3.4 %collective-permute-start.9 = (bf16[192,3,134]{0,2,1:T(8,128)(2,1)S(1)}, bf16[192,3,134]{0,2,1:T(8,128)(2,1)S(1)}, u32[]{:S(2)}, u32[]{:S(2)}) collective-permute-start(bf16[192,3,134]{0,2,1:T(8,128)(2,1)S(1)} %get-tuple-element.480), channel_id=1, source_target_pairs={{0,1},{1,2},{2,3},{4,5},{5,6},{6,7},{8,9},{9,10},{10,11},{12,13},{... | collective-permute-start | bytes 463112 | tf_op jit(solution)/shard_map/ppermute | solution.py:16
  251.7 2.5 collective-permute-done.9
  255.7 16.6 %add_convert_fusion = bf16[192,16,128]{0,2,1:T(8,128)(2,1)S(1)} fusion(bf16[192,16,128]{0,2,1:T(8,128)(2,1)S(1)} %copy-done.14, bf16[192,16,128]{0,2,1:T(8,128)(2,1)S(1)} %bitcast.223, bf16[192,16,3]{0,2,1:T(4,128)(2,1)S(1)} %copy.31, bf16[192,16,3]{0,2,1:T(4,128)(2,1)S(1)} %copy.30, bf16[192,19,134]{0,2,1:T(8,128)(2,1)S(1)} %get-tuple-element.478, ...), kind=kLoop, calls=%fused_computation.266 | loop fusion | flops 66060288 | bytes 35472128 | tf_op jit(solution)/shard_map/convert_element_type | solution.py:199
  273.6 49.7 %all-reduce.3.cloned.1.call-done = (f32[192,768]{1,0:T(8,128)}, f32[768,192]{0,1:T(8,128)}) async-done(((f32[192,768]{1,0:T(8,128)}, f32[768,192]{0,1:T(8,128)}), (f32[192,768]{1,0:T(8,128)}, f32[768,192]{0,1:T(8,128)})) %all-reduce.3.cloned.1.call-update) | async-done | bytes 1179664 | tf_op jit(solution)/shard_map/psum | solution.py:201
  (335 shorter events, 90.1 us)
Async XLA Ops:
  7.2 316.1 %all-reduce.3.cloned.1.call-start = ((), (), s32[]{:S(2)}) async-start(), calls=%async_computation | async-start | bytes 2359296 | tf_op jit(solution)/shard_map/psum | solution.py:201
  9.8 9.6 %collective-permute-start = (bf16[192,16,3]{0,1,2:T(8,128)(2,1)S(1)}, bf16[192,16,3]{0,1,2:T(8,128)(2,1)S(1)}, u32[]{:S(2)}, u32[]{:S(2)}) collective-permute-start(bf16[192,16,3]{0,1,2:T(8,128)(2,1)S(1)} %copy.35), channel_id=1, source_target_pairs={{0,4},{4,8},{8,12},{12,16},{16,20},{20,24},{24,28},{28,0},{1,5},{5... | collective-permute-start | bytes 55304 | tf_op jit(solution)/shard_map/ppermute | solution.py:16
  11.0 8.4 %collective-permute-start.1 = (bf16[192,16,3]{0,1,2:T(8,128)(2,1)S(1)}, bf16[192,16,3]{0,1,2:T(8,128)(2,1)S(1)}, u32[]{:S(2)}, u32[]{:S(2)}) collective-permute-start(bf16[192,16,3]{0,1,2:T(8,128)(2,1)S(1)} %copy.36), channel_id=1, source_target_pairs={{4,0},{8,4},{12,8},{16,12},{20,16},{24,20},{28,24},{0,28},{5,1},{9... | collective-permute-start | bytes 55304 | tf_op jit(solution)/shard_map/ppermute | solution.py:19
  19.5 1.5 collective-permute-start.3
  19.6 20.9 %copy-start.21 = (f32[192,1,1]{0,2,1:T(1,128)}, f32[192,1,1]{0,2,1:T(1,128)S(1)}, u32[]{:S(2)}) copy-start(f32[192,1,1]{0,2,1:T(1,128)S(1)} %get-tuple-element.513) | copy-start | bytes 2308
  19.6 20.9 %copy-start.23 = (f32[192,1,1]{0,2,1:T(1,128)}, f32[192,1,1]{0,2,1:T(1,128)S(1)}, u32[]{:S(2)}) copy-start(f32[192,1,1]{0,2,1:T(1,128)S(1)} %get-tuple-element.514) | copy-start | bytes 2308
  19.7 20.9 %copy-start.25 = (f32[192,1,1]{0,2,1:T(1,128)}, f32[192,1,1]{0,2,1:T(1,128)S(1)}, u32[]{:S(2)}) copy-start(f32[192,1,1]{0,2,1:T(1,128)S(1)} %get-tuple-element.515) | copy-start | bytes 2308
  19.7 20.9 %copy-start.27 = (f32[192,1,1]{0,2,1:T(1,128)}, f32[192,1,1]{0,2,1:T(1,128)S(1)}, u32[]{:S(2)}) copy-start(f32[192,1,1]{0,2,1:T(1,128)S(1)} %get-tuple-element.516) | copy-start | bytes 2308
  19.7 20.9 %copy-start.29 = (f32[192,1,1]{0,2,1:T(1,128)}, f32[192,1,1]{0,2,1:T(1,128)S(1)}, u32[]{:S(2)}) copy-start(f32[192,1,1]{0,2,1:T(1,128)S(1)} %get-tuple-element.517) | copy-start | bytes 2308
  19.7 20.9 %copy-start.31 = (f32[192,1,1]{0,2,1:T(1,128)}, f32[192,1,1]{0,2,1:T(1,128)S(1)}, u32[]{:S(2)}) copy-start(f32[192,1,1]{0,2,1:T(1,128)S(1)} %get-tuple-element.518) | copy-start | bytes 2308
  19.7 20.9 %copy-start.33 = (f32[192,1,1]{0,2,1:T(1,128)}, f32[192,1,1]{0,2,1:T(1,128)S(1)}, u32[]{:S(2)}) copy-start(f32[192,1,1]{0,2,1:T(1,128)S(1)} %get-tuple-element.519) | copy-start | bytes 2308
  19.7 20.9 %copy-start.35 = (f32[192,1,1]{0,2,1:T(1,128)}, f32[192,1,1]{0,2,1:T(1,128)S(1)}, u32[]{:S(2)}) copy-start(f32[192,1,1]{0,2,1:T(1,128)S(1)} %get-tuple-element.520) | copy-start | bytes 2308
  19.7 20.9 %copy-start.37 = (f32[192,1,1]{0,2,1:T(1,128)}, f32[192,1,1]{0,2,1:T(1,128)S(1)}, u32[]{:S(2)}) copy-start(f32[192,1,1]{0,2,1:T(1,128)S(1)} %get-tuple-element.521) | copy-start | bytes 2308
  19.7 20.9 %copy-start.39 = (f32[192,1,1]{0,2,1:T(1,128)}, f32[192,1,1]{0,2,1:T(1,128)S(1)}, u32[]{:S(2)}) copy-start(f32[192,1,1]{0,2,1:T(1,128)S(1)} %get-tuple-element.522) | copy-start | bytes 2308
  19.7 20.9 %copy-start.41 = (f32[192,1,1]{0,2,1:T(1,128)}, f32[192,1,1]{0,2,1:T(1,128)S(1)}, u32[]{:S(2)}) copy-start(f32[192,1,1]{0,2,1:T(1,128)S(1)} %get-tuple-element.523) | copy-start | bytes 2308
  19.7 20.9 %copy-start.43 = (f32[192,1,1]{0,2,1:T(1,128)}, f32[192,1,1]{0,2,1:T(1,128)S(1)}, u32[]{:S(2)}) copy-start(f32[192,1,1]{0,2,1:T(1,128)S(1)} %get-tuple-element.524) | copy-start | bytes 2308
  19.8 20.9 %copy-start.45 = (f32[192,1,1]{0,2,1:T(1,128)}, f32[192,1,1]{0,2,1:T(1,128)S(1)}, u32[]{:S(2)}) copy-start(f32[192,1,1]{0,2,1:T(1,128)S(1)} %get-tuple-element.525) | copy-start | bytes 2308
  19.8 20.9 %copy-start.47 = (f32[192,1,1]{0,2,1:T(1,128)}, f32[192,1,1]{0,2,1:T(1,128)S(1)}, u32[]{:S(2)}) copy-start(f32[192,1,1]{0,2,1:T(1,128)S(1)} %get-tuple-element.526) | copy-start | bytes 2308
  21.0 7.2 %collective-permute-start.4 = (bf16[192,3,134]{0,2,1:T(8,128)(2,1)S(1)}, bf16[192,3,134]{0,2,1:T(8,128)(2,1)S(1)}, u32[]{:S(2)}, u32[]{:S(2)}) collective-permute-start(bf16[192,3,134]{0,2,1:T(8,128)(2,1)S(1)} %collective-permute-done.3), channel_id=1, source_target_pairs={{0,8},{8,0},{4,12},{12,4},{16,24},{24,16},{20,28},{28,20},{1,9},{9... | collective-permute-start | bytes 463112 | tf_op jit(solution)/shard_map/ppermute | solution.py:31
  22.4 18.3 %copy-start.49 = (f32[192,1,1]{0,2,1:T(1,128)}, f32[192,1,1]{0,2,1:T(1,128)S(1)}, u32[]{:S(2)}) copy-start(f32[192,1,1]{0,2,1:T(1,128)S(1)} %get-tuple-element.489) | copy-start | bytes 2308
  22.4 18.3 %copy-start.51 = (f32[192,1,1]{0,2,1:T(1,128)}, f32[192,1,1]{0,2,1:T(1,128)S(1)}, u32[]{:S(2)}) copy-start(f32[192,1,1]{0,2,1:T(1,128)S(1)} %get-tuple-element.490) | copy-start | bytes 2308
  22.4 18.3 %copy-start.53 = (f32[192,1,1]{0,2,1:T(1,128)}, f32[192,1,1]{0,2,1:T(1,128)S(1)}, u32[]{:S(2)}) copy-start(f32[192,1,1]{0,2,1:T(1,128)S(1)} %get-tuple-element.491) | copy-start | bytes 2308
  22.6 13.5 %collective-permute-start.6 = (bf16[192,3,134]{0,2,1:T(8,128)(2,1)S(1)}, bf16[192,3,134]{0,2,1:T(8,128)(2,1)S(1)}, u32[]{:S(2)}, u32[]{:S(2)}) collective-permute-start(bf16[192,3,134]{0,2,1:T(8,128)(2,1)S(1)} %get-tuple-element.483), channel_id=1, source_target_pairs={{1,0},{2,1},{3,2},{5,4},{6,5},{7,6},{9,8},{10,9},{11,10},{13,12},{... | collective-permute-start | bytes 463112 | tf_op jit(solution)/shard_map/ppermute | solution.py:19
  28.3 6.9 %collective-permute-start.5 = (bf16[192,3,134]{0,2,1:T(8,128)(2,1)S(1)}, bf16[192,3,134]{0,2,1:T(8,128)(2,1)S(1)}, u32[]{:S(2)}, u32[]{:S(2)}) collective-permute-start(bf16[192,3,134]{0,2,1:T(8,128)(2,1)S(1)} %collective-permute-done.4), channel_id=1, source_target_pairs={{0,16},{16,0},{4,20},{20,4},{8,24},{24,8},{12,28},{28,12},{1,17},{... | collective-permute-start | bytes 463112 | tf_op jit(solution)/shard_map/ppermute | solution.py:31
  31.2 7.1 %collective-permute-start.2 = (bf16[192,3,134]{0,2,1:T(8,128)(2,1)S(1)}, bf16[192,3,134]{0,2,1:T(8,128)(2,1)S(1)}, u32[]{:S(2)}, u32[]{:S(2)}) collective-permute-start(bf16[192,3,134]{0,2,1:T(8,128)(2,1)S(1)} %get-tuple-element.484), channel_id=1, source_target_pairs={{0,1},{1,2},{2,3},{4,5},{5,6},{6,7},{8,9},{9,10},{10,11},{12,13},{... | collective-permute-start | bytes 463112 | tf_op jit(solution)/shard_map/ppermute | solution.py:16
  158.9 14.7 %collective-permute-start.7 = (bf16[192,16,3]{0,1,2:T(8,128)(2,1)S(1)}, bf16[192,16,3]{0,1,2:T(8,128)(2,1)S(1)}, u32[]{:S(2)}, u32[]{:S(2)}) collective-permute-start(bf16[192,16,3]{0,1,2:T(8,128)(2,1)S(1)} %copy.28), channel_id=1, source_target_pairs={{0,4},{4,8},{8,12},{12,16},{16,20},{20,24},{24,28},{28,0},{1,5},{5... | collective-permute-start | bytes 55304 | tf_op jit(solution)/shard_map/ppermute | solution.py:16
  172.2 1.5 collective-permute-start.8
  173.9 3.0 collective-permute-start.10
  176.9 21.3 %collective-permute-start.11 = (bf16[192,3,134]{0,2,1:T(8,128)(2,1)S(1)}, bf16[192,3,134]{0,2,1:T(8,128)(2,1)S(1)}, u32[]{:S(2)}, u32[]{:S(2)}) collective-permute-start(bf16[192,3,134]{0,2,1:T(8,128)(2,1)S(1)} %collective-permute-done.10), channel_id=1, source_target_pairs={{0,8},{8,0},{4,12},{12,4},{16,24},{24,16},{20,28},{28,20},{1,9},{9... | collective-permute-start | bytes 463112 | tf_op jit(solution)/shard_map/ppermute | solution.py:31
  192.4 58.9 %collective-permute-start.13 = (bf16[192,3,134]{0,2,1:T(8,128)(2,1)S(1)}, bf16[192,3,134]{0,2,1:T(8,128)(2,1)S(1)}, u32[]{:S(2)}, u32[]{:S(2)}) collective-permute-start(bf16[192,3,134]{0,2,1:T(8,128)(2,1)S(1)} %get-tuple-element.479), channel_id=1, source_target_pairs={{1,0},{2,1},{3,2},{5,4},{6,5},{7,6},{9,8},{10,9},{11,10},{13,12},{... | collective-permute-start | bytes 463112 | tf_op jit(solution)/shard_map/ppermute | solution.py:19
  198.2 52.1 %collective-permute-start.12 = (bf16[192,3,134]{0,2,1:T(8,128)(2,1)S(1)}, bf16[192,3,134]{0,2,1:T(8,128)(2,1)S(1)}, u32[]{:S(2)}, u32[]{:S(2)}) collective-permute-start(bf16[192,3,134]{0,2,1:T(8,128)(2,1)S(1)} %collective-permute-done.11), channel_id=1, source_target_pairs={{0,16},{16,0},{4,20},{20,4},{8,24},{24,8},{12,28},{28,12},{1,17},{... | collective-permute-start | bytes 463112 | tf_op jit(solution)/shard_map/ppermute | solution.py:31
  246.8 7.4 %collective-permute-start.9 = (bf16[192,3,134]{0,2,1:T(8,128)(2,1)S(1)}, bf16[192,3,134]{0,2,1:T(8,128)(2,1)S(1)}, u32[]{:S(2)}, u32[]{:S(2)}) collective-permute-start(bf16[192,3,134]{0,2,1:T(8,128)(2,1)S(1)} %get-tuple-element.480), channel_id=1, source_target_pairs={{0,1},{1,2},{2,3},{4,5},{5,6},{6,7},{8,9},{9,10},{10,11},{12,13},{... | collective-permute-start | bytes 463112 | tf_op jit(solution)/shard_map/ppermute | solution.py:16
  (93 other events, 640.5 us)
Sparse Core Ops, SparseCore 0:
  172.4 150.8 all-reduce.2
where the time goes:
time: 336 us; the launch traced here: 334 us
  other arithmetic  84.9 us (25%)
  waiting for transfers between devices  66 us (20%)
  starting transfers between devices  49.5 us (15%)
  blocking collectives  46.7 us (14%)
  local copies, waits for them, and re-layouts  43.6 us (13%)
  matrix products  24.4 us (7%)
  between operations  15.7 us (5%)
    psum x1, waiting for transfers between devices, per_device(): lax.psum((acc_in * factor, acc_out * factor, kernel_local), ('gx', 'gy'))  49.7 us
    psum x1, blocking collectives, per_device(): lax.psum((acc_in * factor, acc_out * factor, kernel_local), ('gx', 'gy'))  46.7 us
    ppermute x6, starting transfers between devices, from_partner(): return lax.ppermute(block, axis, route)  22.9 us
    ppermute x4, starting transfers between devices, padded_2(): lax.ppermute(lax.slice_in_dim(block, block.shape[dim] - width, None, axis...  21 us
    reduce_sum x4, other arithmetic, kernel_terms(): column_sums.append(jnp.sum(grad_float * window, axis=(1, 2)))  19.1 us
    add x1, other arithmetic, depthwise(): summed = summed + weights[:, None, None] * window  17.5 us
    convert_element_type x1, other arithmetic, per_device(): (masked_grad + depthwise(grad_padded, kernel, True)).astype(jnp.bfloat16)  16.6 us
    unnamed x206, local copies, waits for them, and re-layouts  16.2 us
  transfers between devices with their start and end apart: 15, of which 9 were waited for; matrix products, arithmetic and copies ran while one was open for 9% of the time, Pallas kernels for 0%

commit v1 on v0

v1 whole, which is shorter than its diff:
```python
import math

import jax
import jax.numpy as jnp
from jax import lax
from jax.experimental import pallas as pl
from jax.experimental.pallas import tpu as pltpu
from jax.sharding import PartitionSpec as P

ROWS = 4
GROUP = 16
LANES = 128
WIDE = 256
F32 = jnp.float32
BF16 = jnp.bfloat16


def extend(rows):
    height, channels, width = rows.shape
    nx = lax.axis_size("gx")
    ny = lax.axis_size("gy")
    top = rows[height - 3 :]
    bottom = rows[:3]
    south = lax.ppermute(top, "gy", [(i, i + 1) for i in range(ny - 1)])
    north = lax.ppermute(bottom, "gy", [(i + 1, i) for i in range(ny - 1)])
    last = ny - 1
    facing = lax.ppermute(
        top, ("gx", "gy"), [(i * ny + last, (nx - 1 - i) * ny + last) for i in range(nx)]
    )
    turn = jnp.flip(jnp.eye(width, dtype=BF16), 0)
    turned = jnp.dot(facing[::-1].reshape(3 * channels, width), turn, preferred_element_type=F32)
    north = north + turned.astype(BF16).reshape(3, channels, width)
    tall = jnp.concatenate([south, rows, north], axis=0)

    def pack(part):
        return jnp.transpose(part, (0, 2, 1)).reshape((height + 6) * 3, channels)

    def unpack(part):
        return jnp.transpose(part.reshape(height + 6, 3, channels), (0, 2, 1))

    left = lax.ppermute(
        pack(tall[:, :, width - 3 :]), "gx", [(i, (i + 1) % nx) for i in range(nx)]
    )
    right = lax.ppermute(pack(tall[:, :, :3]), "gx", [((i + 1) % nx, i) for i in range(nx)])
    spare = jnp.zeros((height + 6, channels, WIDE - width - 6), BF16)
    return jnp.concatenate([unpack(left), tall, unpack(right), spare], axis=2)


def spread_taps(kernel_ref, taps_ref, flipped):
    table = kernel_ref[...]
    for tap in range(49):
        source = 48 - tap if flipped else tap
        taps_ref[tap] = jnp.broadcast_to(table[:, source : source + 1], taps_ref.shape[1:])


def shift_rows(ext_ref, shifted_ref):
    def one_row(row, carry):
        wide = ext_ref[row].astype(F32)
        for tap in range(7):
            moved = wide if tap == 0 else pltpu.roll(wide, WIDE - tap, 1)
            shifted_ref[tap, row] = moved[:, :LANES]
        return carry

    lax.fori_loop(0, ext_ref.shape[0], one_row, 0)


def conv_group(shifted_ref, taps_ref, first_row, chans):
    sums = [jnp.zeros((GROUP, LANES), F32) for _ in range(ROWS)]
    for col in range(7):
        window = [shifted_ref[col, first_row + r, chans, :] for r in range(ROWS + 6)]
        for row in range(7):
            weight = taps_ref[row * 7 + col, chans, :]
            for i in range(ROWS):
                sums[i] = sums[i] + weight * window[i + row]
    return sums


def gelu_parts(v):
    bell = jnp.exp(v * v * -0.5)
    t = 1.0 / (1.0 + (0.3275911 / math.sqrt(2.0)) * jnp.abs(v))
    poly = t * (
        0.127414796
        + t * (-0.142248368 + t * (0.7107068705 + t * (-0.7265760135 + t * 0.5307027145)))
    )
    tail = poly * bell
    return jnp.where(v < 0.0, tail, 1.0 - tail), bell


def main_kernel(
    ext_ref,
    field_ref,
    cot_ref,
    mask_ref,
    kernel_ref,
    in_ref,
    in_t_ref,
    bias_ref,
    out_ref,
    out_t_ref,
    scale_ref,
    output_ref,
    grad_ref,
    kgrad_ref,
    acc_in_ref,
    acc_out_ref,
    taps_ref,
    shifted_ref,
    kacc_ref,
    conv_ref,
    cgrad_ref,
):
    step = pl.program_id(0)
    channels = conv_ref.shape[0]
    hidden_units = in_ref.shape[1]
    cells = ROWS * LANES
    chunk = 256
    first_row = step * ROWS

    @pl.when(step == 0)
    def _():
        spread_taps(kernel_ref, taps_ref, False)
        shift_rows(ext_ref, shifted_ref)
        kacc_ref[...] = jnp.zeros(kacc_ref.shape, F32)
        acc_in_ref[...] = jnp.zeros(acc_in_ref.shape, F32)
        acc_out_ref[...] = jnp.zeros(acc_out_ref.shape, F32)

    mask = mask_ref[0]
    any_ocean = jnp.max(mask) > 0.0

    @pl.when(jnp.logical_not(any_ocean))
    def _():
        output_ref[...] = jnp.zeros(output_ref.shape, BF16)
        grad_ref[...] = jnp.zeros(grad_ref.shape, BF16)

    @pl.when(any_ocean)
    def _():
        def conv_step(group, carry):
            chans = pl.ds(pl.multiple_of(group * GROUP, GROUP), GROUP)
            sums = conv_group(shifted_ref, taps_ref, first_row, chans)
            for i in range(ROWS):
                conv_ref[chans, i * LANES : (i + 1) * LANES] = sums[i]
            return carry

        lax.fori_loop(0, channels // GROUP, conv_step, 0)

        conv = conv_ref[...]
        centered = conv - jnp.mean(conv, axis=0, keepdims=True)
        variance = jnp.mean(centered * centered, axis=0, keepdims=True)
        inverse = lax.rsqrt(variance + 1e-06)
        normed = centered * inverse
        conv_ref[...] = normed
        normed_half = normed.astype(BF16)
        scale = scale_ref[...]
        cot = jnp.concatenate([cot_ref[i] for i in range(ROWS)], axis=1).astype(F32)
        branch_grad = (scale * (mask * cot)).astype(BF16)
        branch = jnp.zeros((channels, cells), F32)
        normed_grad = jnp.zeros((channels, cells), F32)
        last_dims = (((1,), (1,)), ((), ()))
        for start in range(0, hidden_units, chunk):
            part = slice(start, start + chunk)
            pre_act = (
                jnp.dot(in_t_ref[part, :], normed_half, preferred_element_type=F32)
                + bias_ref[part, :]
            )
            phi, bell = gelu_parts(pre_act)
            hidden = (pre_act * phi).astype(BF16)
            hidden_grad = jnp.dot(out_ref[part, :], branch_grad, preferred_element_type=F32)
            slope = phi + pre_act * bell * (1.0 / math.sqrt(2.0 * math.pi))
            pre_grad = (hidden_grad * slope).astype(BF16)
            branch = branch + jnp.dot(out_t_ref[:, part], hidden, preferred_element_type=F32)
            normed_grad = normed_grad + jnp.dot(
                in_ref[:, part], pre_grad, preferred_element_type=F32
            )
            acc_out_ref[part, :] += lax.dot_general(
                hidden, branch_grad, last_dims, preferred_element_type=F32
            )
            acc_in_ref[:, part] += lax.dot_general(
                normed_half, pre_grad, last_dims, preferred_element_type=F32
            )
        field = jnp.concatenate([field_ref[i] for i in range(ROWS)], axis=1).astype(F32)
        output = (mask * (field + scale * branch)).astype(BF16)
        normed = conv_ref[...]
        mean_grad = jnp.mean(normed_grad, axis=0, keepdims=True)
        mean_prod = jnp.mean(normed_grad * normed, axis=0, keepdims=True)
        conv_grad = (inverse * (normed_grad - mean_grad - normed * mean_prod)).astype(BF16)
        for i in range(ROWS):
            lanes = slice(i * LANES, (i + 1) * LANES)
            output_ref[i] = output[:, lanes]
            grad_ref[i] = conv_grad[:, lanes]
            cgrad_ref[i] = conv_grad[:, lanes].astype(F32)

        def kernel_step(group, carry):
            chans = pl.ds(pl.multiple_of(group * GROUP, GROUP), GROUP)
            grads = [cgrad_ref[i, chans, :] for i in range(ROWS)]
            for col in range(7):
                window = [shifted_ref[col, first_row + r, chans, :] for r in range(ROWS + 6)]
                for row in range(7):
                    total = grads[0] * window[row]
                    for i in range(1, ROWS):
                        total = total + grads[i] * window[i + row]
                    kacc_ref[row * 7 + col, chans, :] += total
            return carry

        lax.fori_loop(0, channels // GROUP, kernel_step, 0)

    @pl.when(step == pl.num_programs(0) - 1)
    def _():
        def reduce_step(group, carry):
            chans = pl.ds(pl.multiple_of(group * GROUP, GROUP), GROUP)
            lane = lax.broadcasted_iota(jnp.int32, (GROUP, LANES), 1)
            table = jnp.zeros((GROUP, LANES), F32)
            for tap in range(49):
                total = jnp.sum(kacc_ref[tap, chans, :], axis=1, keepdims=True)
                table = jnp.where(lane == tap, total, table)
            kgrad_ref[chans, :] = table
            return carry

        lax.fori_loop(0, channels // GROUP, reduce_step, 0)


def field_kernel(ext_ref, cot_ref, mask_ref, kernel_ref, result_ref, taps_ref, shifted_ref):
    step = pl.program_id(0)
    channels = taps_ref.shape[1]
    first_row = step * ROWS

    @pl.when(step == 0)
    def _():
        spread_taps(kernel_ref, taps_ref, True)
        shift_rows(ext_ref, shifted_ref)

    def conv_step(group, carry):
        chans = pl.ds(pl.multiple_of(group * GROUP, GROUP), GROUP)
        sums = conv_group(shifted_ref, taps_ref, first_row, chans)
        for i in range(ROWS):
            mask = mask_ref[0, :, i * LANES : (i + 1) * LANES]
            grad = mask * cot_ref[i, chans, :].astype(F32)
            result_ref[i, chans, :] = (grad + sums[i]).astype(BF16)
        return carry

    lax.fori_loop(0, channels // GROUP, conv_step, 0)


def whole(shape):
    return pl.BlockSpec(shape, lambda step: (0,) * len(shape))


def per_device(
    state_field,
    cotangent,
    ocean_mask,
    kernel,
    inward_weight,
    inward_bias,
    outward_weight,
    layer_scale,
):
    channels, height, width = state_field.shape
    hidden_units = inward_weight.shape[1]
    steps = height // ROWS
    factor = 1.0 / math.sqrt(height * width)
    field = jnp.transpose(state_field, (1, 0, 2))
    cot = jnp.transpose(cotangent, (1, 0, 2))
    mask = ocean_mask.astype(F32).reshape(steps, 1, ROWS * width)
    table = jnp.pad(kernel.reshape(channels, 49), ((0, 0), (0, LANES - 49)))
    ext_shape = (height + 6, channels, WIDE)
    block = pl.BlockSpec((ROWS, channels, width), lambda step: (step, 0, 0))
    mask_block = pl.BlockSpec((1, 1, ROWS * width), lambda step: (step, 0, 0))
    plane = jax.ShapeDtypeStruct((height, channels, width), BF16)
    big = [
        pltpu.VMEM((49, channels, width), F32),
        pltpu.VMEM((7, height + 6, channels, width), F32),
    ]
    params = pltpu.CompilerParams(
        dimension_semantics=("arbitrary",), vmem_limit_bytes=54 * 1024 * 1024
    )
    output, conv_grad, kernel_part, acc_in, acc_out = pl.pallas_call(
        main_kernel,
        grid=(steps,),
        in_specs=[
            whole(ext_shape),
            block,
            block,
            mask_block,
            whole((channels, LANES)),
            whole((channels, hidden_units)),
            whole((hidden_units, channels)),
            whole((hidden_units, 1)),
            whole((hidden_units, channels)),
            whole((channels, hidden_units)),
            whole((channels, 1)),
        ],
        out_specs=[
            block,
            block,
            whole((channels, LANES)),
            whole((channels, hidden_units)),
            whole((hidden_units, channels)),
        ],
        out_shape=[
            plane,
            plane,
            jax.ShapeDtypeStruct((channels, LANES), F32),
            jax.ShapeDtypeStruct((channels, hidden_units), F32),
            jax.ShapeDtypeStruct((hidden_units, channels), F32),
        ],
        scratch_shapes=big
        + [
            pltpu.VMEM((49, channels, width), F32),
            pltpu.VMEM((channels, ROWS * width), F32),
            pltpu.VMEM((ROWS, channels, width), F32),
        ],
        compiler_params=params,
    )(
        extend(field),
        field,
        cot,
        mask,
        table,
        inward_weight,
        inward_weight.T,
        inward_bias[:, None],
        outward_weight,
        outward_weight.T,
        layer_scale[:, None],
    )
    summed = lax.psum((acc_in, acc_out, kernel_part), ("gx", "gy"))
    field_grad = pl.pallas_call(
        field_kernel,
        grid=(steps,),
        in_specs=[whole(ext_shape), block, mask_block, whole((channels, LANES))],
        out_specs=block,
        out_shape=plane,
        scratch_shapes=big,
        compiler_params=params,
        cost_estimate=pl.CostEstimate(
            flops=98 * channels * height * width, bytes_accessed=6000000, transcendentals=0
        ),
    )(extend(conv_grad), cot, mask, table)
    kernel_grad = (summed[2][:, :49] * factor).reshape(channels, 7, 7)
    return (
        jnp.transpose(output, (1, 0, 2)),
        jnp.transpose(field_grad, (1, 0, 2)),
        kernel_grad,
        summed[0] * factor,
        summed[1] * factor,
    )


def solution(mesh):
    in_specs = (P(None, "gy", "gx"), P(None, "gy", "gx"), P("gy", "gx"), P(), P(), P(), P(), P())
    out_specs = (P(None, "gy", "gx"), P(None, "gy", "gx"), P(), P(), P())
    return jax.shard_map(
        per_device, mesh=mesh, in_specs=in_specs, out_specs=out_specs, check_vma=False
    )
```

time: 336 us -> 239 us (0.71)
  other arithmetic: 84.9 us -> 10.1 us
  blocking collectives: 46.7 us -> 0 us
  Pallas kernels: 0 us -> 45 us
  waiting for transfers between devices: 66 us -> 107 us
  matrix products: 24.4 us -> 0.35 us
  local copies, waits for them, and re-layouts: 43.6 us -> 27.2 us
  starting transfers between devices: 49.5 us -> 33.7 us
    psum x1 -> x0, blocking collectives: 46.7 us -> none  [per_device(): lax.psum((acc_in * factor, acc_out * factor, kernel_local), ('gx', 'gy'))]
    psum x1, waiting for transfers between devices: 49.7 us -> 96.3 us  [per_device(): summed = lax.psum((acc_in, acc_out, kernel_part), ('gx', 'gy'))]
    pallas_call x0 -> x2, Pallas kernels: none -> 45 us  [the longest x1 27.4 us: per_device(): pl.pallas_call(main_kernel, grid=(steps,), in_specs=[whole(ext_shape), bl...]
    add x9 -> x2, other arithmetic: 30.7 us -> 0.08 us  [extend(): north = north + turned.astype(BF16).reshape(3, channels, width)]
    reduce_sum x10 -> x0, other arithmetic: 25.5 us -> none  [the longest x4 19.1 us: kernel_terms(): column_sums.append(jnp.sum(grad_float * window, axis=(1, 2)))]
    dot_general x12 -> x2, matrix products: 24.4 us -> 0.35 us  [extend(): jnp.dot(facing[::-1].reshape(3 * channels, width), turn, preferred_elemen...]
    convert_element_type x4 -> x2, other arithmetic: 20.5 us -> 0.61 us  [the longest x1 0.6 us: per_device(): mask = ocean_mask.astype(F32).reshape(steps, 1, ROWS * width)]
    ppermute x14 -> x10, starting transfers between devices: 49.4 us -> 33.7 us  [the longest x2 24.2 us: extend(): south = lax.ppermute(top, 'gy', [(i, i + 1) for i in range(ny - 1)])]
  transfers between devices with their start and end apart: 15 -> 11, of which waited for: 9 -> 3; matrix products, arithmetic and copies ran while one was open for 9% -> 9% of each run, Pallas kernels for 0% -> 7%
where the time goes in v1:
time: 239 us; the launch traced here: 238 us
  waiting for transfers between devices  107 us (45%)
  Pallas kernels  45 us (19%)
  starting transfers between devices  33.7 us (14%)
  local copies, waits for them, and re-layouts  27.2 us (11%)
  between operations  14.4 us (6%)
  other arithmetic  10.1 us (4%)
    psum x1, waiting for transfers between devices, per_device(): summed = lax.psum((acc_in, acc_out, kernel_part), ('gx', 'gy'))  96.3 us
    pallas_call x1, Pallas kernels, per_device(): pl.pallas_call(main_kernel, grid=(steps,), in_specs=[whole(ext_shape), bl...  27.4 us
    ppermute x2, starting transfers between devices, extend(): south = lax.ppermute(top, 'gy', [(i, i + 1) for i in range(ny - 1)])  24.2 us
    pallas_call x1, Pallas kernels, per_device(): pl.pallas_call(field_kernel, grid=(steps,), in_specs=[whole(ext_shape), b...  17.6 us
    ppermute x2, waiting for transfers between devices, extend(): north = lax.ppermute(bottom, 'gy', [(i + 1, i) for i in range(ny - 1)])  11.1 us
    unnamed x29, local copies, waits for them, and re-layouts  10.4 us
    concatenate x2, other arithmetic, extend(): return jnp.concatenate([unpack(left), tall, unpack(right), spare], axis=2)  6.16 us
    ppermute x2, starting transfers between devices, extend(): lax.ppermute(pack(tall[:, :, :3]), 'gx', [((i + 1) % nx, i) for i in rang...  5.5 us
  transfers between devices with their start and end apart: 11, of which 3 were waited for; matrix products, arithmetic and copies ran while one was open for 9% of the time, Pallas kernels for 7%

profile of v1, /device:TPU:0, one launch (start us, length us, event | category | flops | bytes accessed | tf_op | source)
XLA Modules:
  0.0 238.2 jit_solution(7352176950798523740)
XLA Ops:
  7.2 1.3 copy.64
  9.3 4.9 %collective-permute-start = (bf16[3,192,128]{2,1,0:T(8,128)(2,1)S(1)}, bf16[3,192,128]{2,1,0:T(8,128)(2,1)S(1)}, u32[]{:S(2)}, u32[]{:S(2)}) collective-permute-start(bf16[3,192,128]{2,1,0:T(8,128)(2,1)S(1)} %get-tuple-element.39), channel_id=1, source_target_pairs={{0,1},{1,2},{2,3},{4,5},{5,6},{6,7},{8,9},{9,10},{10,11},{12,13},{... | collective-permute-start | bytes 442376 | tf_op jit(solution)/shard_map/ppermute | solution.py:24
  14.2 1.3 collective-permute-start.1
  15.8 5.6 %collective-permute-done.1 = bf16[3,192,128]{2,1,0:T(8,128)(2,1)S(1)} collective-permute-done((bf16[3,192,128]{2,1,0:T(8,128)(2,1)S(1)}, bf16[3,192,128]{2,1,0:T(8,128)(2,1)S(1)}, u32[]{:S(2)}, u32[]{:S(2)}) %collective-permute-start.1) | collective-permute-done | bytes 147488 | tf_op jit(solution)/shard_map/ppermute | solution.py:25
  22.2 1.1 copy.42
  23.3 1.5 reshape.57
  24.8 1.1 copy.44
  26.0 1.4 reshape.59
  27.4 2.6 %collective-permute-start.4 = (bf16[66,192]{1,0:T(8,128)(2,1)}, bf16[66,192]{1,0:T(8,128)(2,1)}, u32[]{:S(2)}, u32[]{:S(2)}) collective-permute-start(bf16[66,192]{1,0:T(8,128)(2,1)} %reshape.59), channel_id=1, source_target_pairs={{4,0},{8,4},{12,8},{16,12},{20,16},{24,20},{28,24},{0,28},{5,1},{9... | collective-permute-start | bytes 76040 | tf_op jit(solution)/shard_map/ppermute | solution.py:44
  30.7 0.8 reshape.62
  31.6 0.8 copy.51.scale_ref
  32.4 0.9 broadcast_in_dim.8.bias_ref
  33.3 0.9 copy.48
  34.2 0.9 copy.50.out_ref
  35.1 1.1 copy.63
  37.0 0.8 reshape.58
  38.4 0.8 reshape.60
  39.9 3.1 %maximum_maximum_fusion.ext_ref = bf16[22,192,256]{2,1,0:T(8,128)(2,1)} fusion(bf16[22,192,3]{2,1,0:T(8,128)(2,1)S(1)} %bitcast.47, bf16[3,192,128]{2,1,0:T(8,128)(2,1)S(1)} %add.14, bf16[16,192,128]{2,1,0:T(8,128)(2,1)S(1)} %bitcast.40, bf16[3,192,128]{2,1,0:T(8,128)(2,1)S(1)} %collective-permute-done, bf16[22,192,3]{2,1,0:T(8,128)(2,1)S(1)} %bitcast.45, ...), kind=kLoop, calls=%fused_computation | loop fusion | flops 12976128 | bytes 3295232 | tf_op jit(solution)/shard_map/concatenate | solution.py:46
  42.9 27.4 %shard_map.119 = (bf16[16,192,128]{2,1,0:T(8,128)(2,1)}, bf16[16,192,128]{2,1,0:T(8,128)(2,1)}, f32[192,128]{1,0:T(8,128)}, f32[192,768]{1,0:T(8,128)}, f32[768,192]{1,0:T(8,128)}) custom-call(bf16[22,192,256]{2,1,0:T(8,128)(2,1)} %maximum_maximum_fusion.ext_ref, bf16[16,192,128]{2,1,0:T(8,128)(2,1)} %bitcast.41, bf16[16,192,128]{2,1,0:T(8,128)(2,1)} %bitcast.42, ...), custom_call_target="tpu_custom_call" | custom-call | tf_op jit(solution)/shard_map/pallas_call | solution.py:276
  70.4 1.1 fusion.1
  72.2 19.2 %collective-permute-start.5 = (bf16[3,192,128]{2,1,0:T(8,128)(2,1)S(1)}, bf16[3,192,128]{2,1,0:T(8,128)(2,1)S(1)}, u32[]{:S(2)}, u32[]{:S(2)}) collective-permute-start(bf16[3,192,128]{2,1,0:T(8,128)(2,1)S(1)} %get-tuple-element.37), channel_id=1, source_target_pairs={{0,1},{1,2},{2,3},{4,5},{5,6},{6,7},{8,9},{9,10},{10,11},{12,13},{... | collective-permute-start | bytes 442376 | tf_op jit(solution)/shard_map/ppermute | solution.py:24
  91.4 1.3 collective-permute-start.6
  92.9 5.5 %collective-permute-done.6 = bf16[3,192,128]{2,1,0:T(8,128)(2,1)S(1)} collective-permute-done((bf16[3,192,128]{2,1,0:T(8,128)(2,1)S(1)}, bf16[3,192,128]{2,1,0:T(8,128)(2,1)S(1)}, u32[]{:S(2)}, u32[]{:S(2)}) %collective-permute-start.6) | collective-permute-done | bytes 147488 | tf_op jit(solution)/shard_map/ppermute | solution.py:25
  100.3 2.9 %collective-permute-start.9 = (bf16[66,192]{1,0:T(8,128)(2,1)S(1)}, bf16[66,192]{1,0:T(8,128)(2,1)S(1)}, u32[]{:S(2)}, u32[]{:S(2)}) collective-permute-start(bf16[66,192]{1,0:T(8,128)(2,1)S(1)} %reshape.67), channel_id=1, source_target_pairs={{4,0},{8,4},{12,8},{16,12},{20,16},{24,20},{28,24},{0,28},{5,1},{9... | collective-permute-start | bytes 76040 | tf_op jit(solution)/shard_map/ppermute | solution.py:44
  103.2 2.5 %copy.58 = bf16[192,16,128]{2,1,0:T(8,128)(2,1)} copy(bf16[192,16,128]{2,0,1:T(8,128)(2,1)} %bitcast.51) | data formatting | bytes 1572864
  107.1 3.1 %maximum_maximum_fusion.1.ext_ref = bf16[22,192,256]{2,1,0:T(8,128)(2,1)} fusion(bf16[22,192,3]{2,1,0:T(8,128)(2,1)S(1)} %bitcast.46, bf16[3,192,128]{2,1,0:T(8,128)(2,1)S(1)} %add.15, bf16[16,192,128]{2,1,0:T(8,128)(2,1)S(1)} %copy-done.1, bf16[3,192,128]{2,1,0:T(8,128)(2,1)S(1)} %collective-permute-done.5, bf16[22,192,3]{2,1,0:T(8,128)(2,1)S(1)} %bitcast.44, ...), kind=kLoop, calls=%fused_computation.1 | loop fusion | flops 12976128 | bytes 3295232 | tf_op jit(solution)/shard_map/concatenate | solution.py:46
  110.2 17.6 %shard_map.120 = bf16[16,192,128]{2,1,0:T(8,128)(2,1)} custom-call(bf16[22,192,256]{2,1,0:T(8,128)(2,1)} %maximum_maximum_fusion.1.ext_ref, bf16[16,192,128]{2,1,0:T(8,128)(2,1)} %bitcast.43, f32[4,1,512]{2,1,0:T(1,128)} %bitcast.57, f32[192,128]{1,0:T(8,128)} %pad.4.kernel_ref), custom_call_target="tpu_custom_call" | custom-call | flops 38535168 | bytes 6000000 | tf_op jit(solution)/shard_map/pallas_call | solution.py:327
  127.7 2.5 %copy.59 = bf16[192,16,128]{2,1,0:T(8,128)(2,1)} copy(bf16[192,16,128]{2,0,1:T(8,128)(2,1)} %bitcast.48) | data formatting | bytes 1572864
  130.3 96.3 %all-reduce.4.cloned.1.call-done = (f32[192,128]{1,0:T(8,128)}, f32[192,768]{1,0:T(8,128)}, f32[768,192]{1,0:T(8,128)}) async-done(((f32[192,128]{1,0:T(8,128)}, f32[192,768]{1,0:T(8,128)}, f32[768,192]{1,0:T(8,128)}), (f32[192,128]{1,0:T(8,128)}, f32[192,768]{1,0:T(8,128)}, f32[768,192]{1,0:T(8,128)})) %all-reduce.4.cloned.1.call-update) | async-done | bytes 1277968 | tf_op jit(solution)/shard_map/psum | solution.py:326
  226.6 1.0 slice_multiply_fusion
  228.3 1.9 broadcast_multiply_fusion.1
  230.3 1.1 copy.60
  (67 shorter events, 9.3 us)
Async XLA Ops:
  7.2 219.4 %all-reduce.4.cloned.1.call-start = ((), (), s32[]{:S(2)}) async-start(), calls=%async_computation | async-start | bytes 2949120 | tf_op jit(solution)/shard_map/psum | solution.py:326
  8.6 31.3 %copy-start = (bf16[192,16,128]{2,0,1:T(8,128)(2,1)}, bf16[192,16,128]{2,0,1:T(8,128)(2,1)S(1)}, u32[]{:S(2)}) copy-start(bf16[192,16,128]{2,0,1:T(8,128)(2,1)S(1)} %copy.64) | copy-start | bytes 2359300
  8.6 7.0 %collective-permute-start.2 = (bf16[3,192,128]{2,1,0:T(8,128)(2,1)S(1)}, bf16[3,192,128]{2,1,0:T(8,128)(2,1)S(1)}, u32[]{:S(2)}, u32[]{:S(2)}) collective-permute-start(bf16[3,192,128]{2,1,0:T(8,128)(2,1)S(1)} %get-tuple-element.39), channel_id=1, source_target_pairs={{3,31},{7,27},{11,23},{15,19},{19,15},{23,11},{27,7},{31,3}} | collective-permute-start | bytes 442376 | tf_op jit(solution)/shard_map/ppermute | solution.py:27
  9.3 12.2 %collective-permute-start = (bf16[3,192,128]{2,1,0:T(8,128)(2,1)S(1)}, bf16[3,192,128]{2,1,0:T(8,128)(2,1)S(1)}, u32[]{:S(2)}, u32[]{:S(2)}) collective-permute-start(bf16[3,192,128]{2,1,0:T(8,128)(2,1)S(1)} %get-tuple-element.39), channel_id=1, source_target_pairs={{0,1},{1,2},{2,3},{4,5},{5,6},{6,7},{8,9},{9,10},{10,11},{12,13},{... | collective-permute-start | bytes 442376 | tf_op jit(solution)/shard_map/ppermute | solution.py:24
  14.2 7.2 %collective-permute-start.1 = (bf16[3,192,128]{2,1,0:T(8,128)(2,1)S(1)}, bf16[3,192,128]{2,1,0:T(8,128)(2,1)S(1)}, u32[]{:S(2)}, u32[]{:S(2)}) collective-permute-start(bf16[3,192,128]{2,1,0:T(8,128)(2,1)S(1)} %get-tuple-element.40), channel_id=1, source_target_pairs={{1,0},{2,1},{3,2},{5,4},{6,5},{7,6},{9,8},{10,9},{11,10},{13,12},{... | collective-permute-start | bytes 442376 | tf_op jit(solution)/shard_map/ppermute | solution.py:25
  15.6 5.9 %copy-start.6 = (bf16[128,128]{1,0:T(8,128)(2,1)}, bf16[128,128]{1,0:T(8,128)(2,1)S(1)}, u32[]{:S(2)}) copy-start(bf16[128,128]{1,0:T(8,128)(2,1)S(1)} %rev.11) | copy-start | bytes 98308
  22.1 7.9 %copy-start.8 = (s32[16,128]{1,0:T(8,128)S(1)}, s32[16,128]{1,0:T(8,128)}, u32[]{:S(2)}) copy-start(s32[16,128]{1,0:T(8,128)} %param.10) | copy-start | bytes 24580
  22.1 9.5 %copy-start.10 = (f32[192]{0:T(256)S(1)}, f32[192]{0:T(256)}, u32[]{:S(2)}) copy-start(f32[192]{0:T(256)} %param.15) | copy-start | bytes 2308
  22.1 10.2 %copy-start.9 = (f32[768]{0:T(1024)S(1)}, f32[768]{0:T(1024)}, u32[]{:S(2)}) copy-start(f32[768]{0:T(1024)} %param.13) | copy-start | bytes 9220
  22.2 11.1 %copy-start.2 = (bf16[192,768]{1,0:T(8,128)(2,1)S(1)}, bf16[192,768]{1,0:T(8,128)(2,1)}, u32[]{:S(2)}) copy-start(bf16[192,768]{1,0:T(8,128)(2,1)} %in_ref.1) | copy-start | bytes 884740
  23.3 10.9 %copy-start.3 = (bf16[768,192]{0,1:T(8,128)(2,1)S(1)}, bf16[768,192]{0,1:T(8,128)(2,1)}, u32[]{:S(2)}) copy-start(bf16[768,192]{0,1:T(8,128)(2,1)} %param.14) | copy-start | bytes 884740
  23.3 11.8 %copy-start.4 = (bf16[192,16,128]{2,1,0:T(8,128)(2,1)S(1)}, bf16[192,16,128]{2,1,0:T(8,128)(2,1)}, u32[]{:S(2)}) copy-start(bf16[192,16,128]{2,1,0:T(8,128)(2,1)} %param.9) | copy-start | bytes 2359300
  24.8 12.1 %collective-permute-start.3 = (bf16[66,192]{1,0:T(8,128)(2,1)}, bf16[66,192]{1,0:T(8,128)(2,1)}, u32[]{:S(2)}, u32[]{:S(2)}) collective-permute-start(bf16[66,192]{1,0:T(8,128)(2,1)} %reshape.57), channel_id=1, source_target_pairs={{0,4},{4,8},{8,12},{12,16},{16,20},{20,24},{24,28},{28,0},{1,5},{5... | collective-permute-start | bytes 76040 | tf_op jit(solution)/shard_map/ppermute | solution.py:41
  27.4 11.0 %collective-permute-start.4 = (bf16[66,192]{1,0:T(8,128)(2,1)}, bf16[66,192]{1,0:T(8,128)(2,1)}, u32[]{:S(2)}, u32[]{:S(2)}) collective-permute-start(bf16[66,192]{1,0:T(8,128)(2,1)} %reshape.59), channel_id=1, source_target_pairs={{4,0},{8,4},{12,8},{16,12},{20,16},{24,20},{28,24},{0,28},{5,1},{9... | collective-permute-start | bytes 76040 | tf_op jit(solution)/shard_map/ppermute | solution.py:44
  70.4 22.4 %copy-start.7 = (bf16[128,128]{1,0:T(8,128)(2,1)S(1)}, bf16[128,128]{1,0:T(8,128)(2,1)}, u32[]{:S(2)}) copy-start(bf16[128,128]{1,0:T(8,128)(2,1)} %copy-done.6) | copy-start | bytes 98308
  70.4 28.1 %copy-start.1 = (bf16[16,192,128]{2,1,0:T(8,128)(2,1)S(1)}, bf16[16,192,128]{2,1,0:T(8,128)(2,1)}, u32[]{:S(2)}) copy-start(bf16[16,192,128]{2,1,0:T(8,128)(2,1)} %get-tuple-element.11) | copy-start | bytes 2359300
  71.5 21.2 %collective-permute-start.7 = (bf16[3,192,128]{2,1,0:T(8,128)(2,1)S(1)}, bf16[3,192,128]{2,1,0:T(8,128)(2,1)S(1)}, u32[]{:S(2)}, u32[]{:S(2)}) collective-permute-start(bf16[3,192,128]{2,1,0:T(8,128)(2,1)S(1)} %get-tuple-element.37), channel_id=1, source_target_pairs={{3,31},{7,27},{11,23},{15,19},{19,15},{23,11},{27,7},{31,3}} | collective-permute-start | bytes 442376 | tf_op jit(solution)/shard_map/ppermute | solution.py:27
  72.2 26.3 %collective-permute-start.5 = (bf16[3,192,128]{2,1,0:T(8,128)(2,1)S(1)}, bf16[3,192,128]{2,1,0:T(8,128)(2,1)S(1)}, u32[]{:S(2)}, u32[]{:S(2)}) collective-permute-start(bf16[3,192,128]{2,1,0:T(8,128)(2,1)S(1)} %get-tuple-element.37), channel_id=1, source_target_pairs={{0,1},{1,2},{2,3},{4,5},{5,6},{6,7},{8,9},{9,10},{10,11},{12,13},{... | collective-permute-start | bytes 442376 | tf_op jit(solution)/shard_map/ppermute | solution.py:24
  91.4 7.0 %collective-permute-start.6 = (bf16[3,192,128]{2,1,0:T(8,128)(2,1)S(1)}, bf16[3,192,128]{2,1,0:T(8,128)(2,1)S(1)}, u32[]{:S(2)}, u32[]{:S(2)}) collective-permute-start(bf16[3,192,128]{2,1,0:T(8,128)(2,1)S(1)} %get-tuple-element.38), channel_id=1, source_target_pairs={{1,0},{2,1},{3,2},{5,4},{6,5},{7,6},{9,8},{10,9},{11,10},{13,12},{... | collective-permute-start | bytes 442376 | tf_op jit(solution)/shard_map/ppermute | solution.py:25
  99.7 6.0 %collective-permute-start.8 = (bf16[66,192]{1,0:T(8,128)(2,1)S(1)}, bf16[66,192]{1,0:T(8,128)(2,1)S(1)}, u32[]{:S(2)}, u32[]{:S(2)}) collective-permute-start(bf16[66,192]{1,0:T(8,128)(2,1)S(1)} %reshape.65), channel_id=1, source_target_pairs={{0,4},{4,8},{8,12},{12,16},{16,20},{20,24},{24,28},{28,0},{1,5},{5... | collective-permute-start | bytes 76040 | tf_op jit(solution)/shard_map/ppermute | solution.py:41
  100.3 6.1 %collective-permute-start.9 = (bf16[66,192]{1,0:T(8,128)(2,1)S(1)}, bf16[66,192]{1,0:T(8,128)(2,1)S(1)}, u32[]{:S(2)}, u32[]{:S(2)}) collective-permute-start(bf16[66,192]{1,0:T(8,128)(2,1)S(1)} %reshape.67), channel_id=1, source_target_pairs={{4,0},{8,4},{12,8},{16,12},{20,16},{24,20},{28,24},{0,28},{5,1},{9... | collective-permute-start | bytes 76040 | tf_op jit(solution)/shard_map/ppermute | solution.py:44
  226.6 3.6 %copy-start.5 = (f32[768,192]{1,0:T(8,128)S(1)}, f32[768,192]{1,0:T(8,128)}, u32[]{:S(2)}) copy-start(f32[768,192]{1,0:T(8,128)} %get-tuple-element.32) | copy-start | bytes 1769476
Sparse Core Ops, SparseCore 0:
  92.8 133.6 all-reduce.3

commit v2 on v1

--- a/solution.py
+++ b/solution.py
@@ -1,3 +1,4 @@
+import functools
 import math
 
 import jax
@@ -100,9 +101,7 @@
     scale_ref,
     output_ref,
     grad_ref,
-    kgrad_ref,
-    acc_in_ref,
-    acc_out_ref,
+    acc_ref,
     taps_ref,
     shifted_ref,
     kacc_ref,
@@ -121,8 +120,7 @@
         spread_taps(kernel_ref, taps_ref, False)
         shift_rows(ext_ref, shifted_ref)
         kacc_ref[...] = jnp.zeros(kacc_ref.shape, F32)
-        acc_in_ref[...] = jnp.zeros(acc_in_ref.shape, F32)
-        acc_out_ref[...] = jnp.zeros(acc_out_ref.shape, F32)
+        acc_ref[...] = jnp.zeros(acc_ref.shape, F32)
 
     mask = mask_ref[0]
     any_ocean = jnp.max(mask) > 0.0
@@ -171,12 +169,16 @@
             normed_grad = normed_grad + jnp.dot(
                 in_ref[:, part], pre_grad, preferred_element_type=F32
             )
-            acc_out_ref[part, :] += lax.dot_general(
-                hidden, branch_grad, last_dims, preferred_element_type=F32
-            )
-            acc_in_ref[:, part] += lax.dot_general(
+            in_part = lax.dot_general(
                 normed_half, pre_grad, last_dims, preferred_element_type=F32
             )
+            out_part = lax.dot_general(
+                branch_grad, hidden, last_dims, preferred_element_type=F32
+            )
+            for first, value in ((0, in_part), (hidden_units // LANES, out_part)):
+                for k in range(chunk // LANES):
+                    at = (first + start // LANES + k) * channels
+                    acc_ref[at : at + channels, :] += value[:, k * LANES : (k + 1) * LANES]
         field = jnp.concatenate([field_ref[i] for i in range(ROWS)], axis=1).astype(F32)
         output = (mask * (field + scale * branch)).astype(BF16)
         normed = conv_ref[...]
@@ -212,7 +214,8 @@
             for tap in range(49):
                 total = jnp.sum(kacc_ref[tap, chans, :], axis=1, keepdims=True)
                 table = jnp.where(lane == tap, total, table)
-            kgrad_ref[chans, :] = table
+            at = 2 * (hidden_units // LANES) * channels + group * GROUP
+            acc_ref[pl.ds(pl.multiple_of(at, GROUP), GROUP), :] = table
             return carry
 
         lax.fori_loop(0, channels // GROUP, reduce_step, 0)
@@ -238,6 +241,83 @@
         return carry
 
     lax.fori_loop(0, channels // GROUP, conv_step, 0)
+
+
+def sum_kernel(route, factor, part_ref, result_ref, held_ref, final_ref, *rest):
+    count = len(route)
+    inbox = rest[:count]
+    send_sem, recv_sem, back_send_sem, back_recv_sem = rest[count:]
+    partners = []
+    for axis, bit in route:
+        me = lax.axis_index(axis)
+        mine = (me // (1 << bit)) % 2
+        partners.append((mine, {axis: me + (1 - 2 * mine) * (1 << bit)}))
+    barrier = pltpu.get_barrier_semaphore()
+    for _, target in partners:
+        pl.semaphore_signal(
+            barrier, inc=1, device_id=target, device_id_type=pl.DeviceIdType.MESH
+        )
+    pl.semaphore_wait(barrier, count)
+
+    base = 0
+    size = part_ref.shape[0]
+    source = part_ref
+    for k, (mine, target) in enumerate(partners):
+        size = size // 2
+        keep = pl.ds(pl.multiple_of(base + mine * size, 16), size)
+        give = pl.ds(pl.multiple_of(base + (1 - mine) * size, 16), size)
+        copy = pltpu.make_async_remote_copy(
+            src_ref=source.at[give],
+            dst_ref=inbox[k],
+            send_sem=send_sem.at[k],
+            recv_sem=recv_sem.at[k],
+            device_id=target,
+            device_id_type=pl.DeviceIdType.MESH,
+        )
+        copy.start()
+        copy.wait()
+        held_ref[keep, :] = source[keep, :] + inbox[k][...]
+        source = held_ref
+        base = base + mine * size
+    own = pl.ds(pl.multiple_of(base, 16), size)
+    final_ref[own, :] = (held_ref[own, :] * factor).astype(BF16)
+    for k in reversed(range(count)):
+        mine, target = partners[k]
+        block = pl.ds(pl.multiple_of(base, 16), size)
+        copy = pltpu.make_async_remote_copy(
+            src_ref=final_ref.at[block],
+            dst_ref=final_ref.at[block],
+            send_sem=back_send_sem.at[k],
+            recv_sem=back_recv_sem.at[k],
+            device_id=target,
+            device_id_type=pl.DeviceIdType.MESH,
+        )
+        copy.start()
+        copy.wait()
+        base = base - mine * size
+        size = size * 2
+    result_ref[...] = final_ref[...].astype(F32)
+
+
+def sum_devices(part, factor):
+    route = []
+    for axis in ("gx", "gy"):
+        bits = lax.axis_size(axis).bit_length() - 1
+        route += [(axis, bit) for bit in range(bits)]
+    rows = part.shape[0]
+    count = len(route)
+    return pl.pallas_call(
+        functools.partial(sum_kernel, tuple(route), factor),
+        in_specs=[pl.BlockSpec(memory_space=pltpu.VMEM)],
+        out_specs=pl.BlockSpec(memory_space=pltpu.VMEM),
+        out_shape=jax.ShapeDtypeStruct(part.shape, F32),
+        scratch_shapes=[pltpu.VMEM(part.shape, F32), pltpu.VMEM(part.shape, BF16)]
+        + [pltpu.VMEM((rows >> (k + 1), LANES), F32) for k in range(count)]
+        + [pltpu.SemaphoreType.DMA((count,))] * 4,
+        compiler_params=pltpu.CompilerParams(
+            collective_id=0, has_side_effects=True, vmem_limit_bytes=24 * 1024 * 1024
+        ),
+    )(part)
 
 
 def whole(shape):
@@ -273,7 +353,11 @@
     params = pltpu.CompilerParams(
         dimension_semantics=("arbitrary",), vmem_limit_bytes=54 * 1024 * 1024
     )
-    output, conv_grad, kernel_part, acc_in, acc_out = pl.pallas_call(
+    blocks = hidden_units // LANES
+    used = (2 * blocks + 1) * channels
+    share = GROUP * lax.axis_size("gx") * lax.axis_size("gy")
+    total = -(-used // share) * share
+    output, conv_grad, acc = pl.pallas_call(
         main_kernel,
         grid=(steps,),
         in_specs=[
@@ -292,16 +376,12 @@
         out_specs=[
             block,
             block,
-            whole((channels, LANES)),
-            whole((channels, hidden_units)),
-            whole((hidden_units, channels)),
+            whole((total, LANES)),
         ],
         out_shape=[
             plane,
             plane,
-            jax.ShapeDtypeStruct((channels, LANES), F32),
-            jax.ShapeDtypeStruct((channels, hidden_units), F32),
-            jax.ShapeDtypeStruct((hidden_units, channels), F32),
+            jax.ShapeDtypeStruct((total, LANES), F32),
         ],
         scratch_shapes=big
         + [
@@ -323,7 +403,11 @@
         outward_weight.T,
         layer_scale[:, None],
     )
-    summed = lax.psum((acc_in, acc_out, kernel_part), ("gx", "gy"))
+    summed = sum_devices(acc, factor)[:used].reshape(2 * blocks + 1, channels, LANES)
+    inward_grad = jnp.transpose(summed[:blocks], (1, 0, 2)).reshape(channels, hidden_units)
+    outward_grad = jnp.transpose(summed[blocks : 2 * blocks], (0, 2, 1)).reshape(
+        hidden_units, channels
+    )
     field_grad = pl.pallas_call(
         field_kernel,
         grid=(steps,),
@@ -336,13 +420,13 @@
             flops=98 * channels * height * width, bytes_accessed=6000000, transcendentals=0
         ),
     )(extend(conv_grad), cot, mask, table)
-    kernel_grad = (summed[2][:, :49] * factor).reshape(channels, 7, 7)
+    kernel_grad = summed[2 * blocks, :, :49].reshape(channels, 7, 7)
     return (
         jnp.transpose(output, (1, 0, 2)),
         jnp.transpose(field_grad, (1, 0, 2)),
         kernel_grad,
-        summed[0] * factor,
-        summed[1] * factor,
+        inward_grad,
+        outward_grad,
     )
 
 

time: 239 us -> 169 us (0.71)
  waiting for transfers between devices: 107 us -> 5.66 us
  Pallas kernels: 45 us -> 106 us
  starting transfers between devices: 33.7 us -> 13.5 us
  between operations: 14.4 us -> 1.04 us
  local copies, waits for them, and re-layouts: 27.2 us -> 33.9 us
  other arithmetic: 10.1 us -> 7.09 us
    psum x1 -> x0, waiting for transfers between devices: 96.3 us -> none  [per_device(): summed = lax.psum((acc_in, acc_out, kernel_part), ('gx', 'gy'))]
    pallas_call x0 -> x1, Pallas kernels: none -> 54.7 us  [sum_devices(): pl.pallas_call(functools.partial(sum_kernel, tuple(route), factor), in_sp...]
    ppermute x2, starting transfers between devices: 24.2 us -> 6.23 us  [extend(): south = lax.ppermute(top, 'gy', [(i, i + 1) for i in range(ny - 1)])]
    pallas_call x1, Pallas kernels: 27.4 us -> 34.2 us  [per_device(): pl.pallas_call(main_kernel, grid=(steps,), in_specs=[whole(ext_shape), bl...]
    ppermute x2, waiting for transfers between devices: 11.1 us -> 5.64 us  [extend(): north = lax.ppermute(bottom, 'gy', [(i + 1, i) for i in range(ny - 1)])]
    mul x3 -> x0, other arithmetic: 2.97 us -> none  [the longest x1 1.93 us: per_device(): summed[0] * factor]
    ppermute x2, starting transfers between devices: 5.5 us -> 2.7 us  [extend(): lax.ppermute(pack(tall[:, :, :3]), 'gx', [((i + 1) % nx, i) for i in rang...]
    slice x0 -> x5, local copies, waits for them, and re-layouts: none -> 2.67 us  [the longest x2 1.31 us: per_device(): summed[blocks:2 * blocks]]
  transfers between devices with their start and end apart: 11 -> 10, of which waited for: 3 -> 1; matrix products, arithmetic and copies ran while one was open for 9% -> 12% of each run, Pallas kernels for 7% -> 33%
where the time goes in v2:
time: 169 us; the launch traced here: 168 us
  Pallas kernels  106 us (63%)
  local copies, waits for them, and re-layouts  33.9 us (20%)
  starting transfers between devices  13.5 us (8%)
  other arithmetic  7.09 us (4%)
  waiting for transfers between devices  5.66 us (3%)
    pallas_call x1, Pallas kernels, sum_devices(): pl.pallas_call(functools.partial(sum_kernel, tuple(route), factor), in_sp...  54.7 us
    pallas_call x1, Pallas kernels, per_device(): pl.pallas_call(main_kernel, grid=(steps,), in_specs=[whole(ext_shape), bl...  34.2 us
    pallas_call x1, Pallas kernels, per_device(): pl.pallas_call(field_kernel, grid=(steps,), in_specs=[whole(ext_shape), b...  17.5 us
    unnamed x35, local copies, waits for them, and re-layouts  9.7 us
    transpose x6, local copies, waits for them, and re-layouts, pack(): return jnp.transpose(part, (0, 2, 1)).reshape((height + 6) * 3, channels)  6.51 us
    ppermute x2, starting transfers between devices, extend(): south = lax.ppermute(top, 'gy', [(i, i + 1) for i in range(ny - 1)])  6.23 us
    concatenate x2, other arithmetic, extend(): return jnp.concatenate([unpack(left), tall, unpack(right), spare], axis=2)  6.13 us
    ppermute x2, waiting for transfers between devices, extend(): north = lax.ppermute(bottom, 'gy', [(i + 1, i) for i in range(ny - 1)])  5.64 us
  transfers between devices with their start and end apart: 10, of which 1 were waited for; matrix products, arithmetic and copies ran while one was open for 12% of the time, Pallas kernels for 33%

profile of v2, /device:TPU:0, one launch (start us, length us, event | category | flops | bytes accessed | tf_op | source)
XLA Modules:
  0.0 167.9 jit_solution(8234681464096851203)
XLA Ops:
  0.6 1.3 copy.51
  2.7 4.9 %collective-permute-start = (bf16[3,192,128]{2,1,0:T(8,128)(2,1)S(1)}, bf16[3,192,128]{2,1,0:T(8,128)(2,1)S(1)}, u32[]{:S(2)}, u32[]{:S(2)}) collective-permute-start(bf16[3,192,128]{2,1,0:T(8,128)(2,1)S(1)} %get-tuple-element.29), channel_id=1, source_target_pairs={{0,1},{1,2},{2,3},{4,5},{5,6},{6,7},{8,9},{9,10},{10,11},{12,13},{... | collective-permute-start | bytes 442376 | tf_op jit(solution)/shard_map/ppermute | solution.py:25
  7.6 1.3 collective-permute-start.1
  9.2 5.6 %collective-permute-done.1 = bf16[3,192,128]{2,1,0:T(8,128)(2,1)S(1)} collective-permute-done((bf16[3,192,128]{2,1,0:T(8,128)(2,1)S(1)}, bf16[3,192,128]{2,1,0:T(8,128)(2,1)S(1)}, u32[]{:S(2)}, u32[]{:S(2)}) %collective-permute-start.1) | collective-permute-done | bytes 147488 | tf_op jit(solution)/shard_map/ppermute | solution.py:26
  15.6 1.1 copy.24
  16.7 1.5 reshape.65
  18.3 1.1 copy.26
  19.4 1.4 reshape.67
  20.8 2.6 %collective-permute-start.4 = (bf16[66,192]{1,0:T(8,128)(2,1)}, bf16[66,192]{1,0:T(8,128)(2,1)}, u32[]{:S(2)}, u32[]{:S(2)}) collective-permute-start(bf16[66,192]{1,0:T(8,128)(2,1)} %reshape.67), channel_id=1, source_target_pairs={{4,0},{8,4},{12,8},{16,12},{20,16},{24,20},{28,24},{0,28},{5,1},{9... | collective-permute-start | bytes 76040 | tf_op jit(solution)/shard_map/ppermute | solution.py:45
  24.1 0.8 reshape.70
  25.8 0.9 broadcast_in_dim.8.bias_ref
  26.7 0.9 copy.30
  27.6 1.0 copy.32.out_ref
  28.6 1.1 copy.50
  30.4 0.8 reshape.66
  31.9 0.8 reshape.68
  33.3 3.1 %maximum_maximum_fusion.ext_ref = bf16[22,192,256]{2,1,0:T(8,128)(2,1)} fusion(bf16[22,192,3]{2,1,0:T(8,128)(2,1)S(1)} %bitcast.60, bf16[3,192,128]{2,1,0:T(8,128)(2,1)S(1)} %add.8, bf16[16,192,128]{2,1,0:T(8,128)(2,1)S(1)} %bitcast.53, bf16[3,192,128]{2,1,0:T(8,128)(2,1)S(1)} %collective-permute-done, bf16[22,192,3]{2,1,0:T(8,128)(2,1)S(1)} %bitcast.58, ...), kind=kLoop, calls=%fused_computation | loop fusion | flops 12976128 | bytes 3295232 | tf_op jit(solution)/shard_map/concatenate | solution.py:47
  36.4 34.2 %shard_map.119 = (bf16[16,192,128]{2,1,0:T(8,128)(2,1)}, bf16[16,192,128]{2,1,0:T(8,128)(2,1)}, f32[2560,128]{1,0:T(8,128)}) custom-call(bf16[22,192,256]{2,1,0:T(8,128)(2,1)} %maximum_maximum_fusion.ext_ref, bf16[16,192,128]{2,1,0:T(8,128)(2,1)} %bitcast.54, bf16[16,192,128]{2,1,0:T(8,128)(2,1)} %bitcast.55, f32[4,1,512]{2,1,0:T(1,128)} %bitcast.74, ...), custom_call_target="tpu_custom_call" | custom-call | tf_op jit(solution)/shard_map/pallas_call | solution.py:360
  70.6 1.0 fusion.2
  72.3 1.3 collective-permute-start.5
  73.6 1.5 collective-permute-start.6
  75.1 1.3 copy-done
  76.4 54.7 %shard_map.121 = f32[2560,128]{1,0:T(8,128)S(1)} custom-call(f32[2560,128]{1,0:T(8,128)S(1)} %copy-done), custom_call_target="tpu_custom_call" | custom-call | tf_op jit(solution)/shard_map/pallas_call | solution.py:309
  131.2 1.3 copy.39
  132.4 1.2 copy.40
  134.1 1.5 slice_bitcast_fusion.1
  135.6 1.7 %copy.34 = bf16[22,3,192]{2,1,0:T(4,128)(2,1)S(1)} copy(bf16[22,3,192]{1,2,0:T(8,128)(2,1)} %get-tuple-element.23) | data formatting | bytes 50688 | tf_op jit(solution)/shard_map/transpose | solution.py:37
  138.5 2.7 %copy_bitcast_fusion.2 = (f32[768,192]{0,1:T(8,128)}, f32[192,768]{1,0:T(8,128)}) fusion(f32[24,8,6,128]{3,2,1,0:T(8,128)} %bitcast.62, f32[24,8,6,128]{3,2,1,0:T(8,128)} %bitcast.61), kind=kLoop, calls=%fused_computation.12 | loop fusion | bytes 2359296 | tf_op jit(solution)/shard_map/reshape | solution.py:408
  141.3 1.4 copy.41
  144.8 3.1 %maximum_maximum_fusion.1.ext_ref = bf16[22,192,256]{2,1,0:T(8,128)(2,1)} fusion(bf16[22,192,3]{2,1,0:T(8,128)(2,1)S(1)} %bitcast.59, bf16[3,192,128]{2,1,0:T(8,128)(2,1)S(1)} %add.9, bf16[16,192,128]{2,1,0:T(8,128)(2,1)S(1)} %copy-done.2, bf16[3,192,128]{2,1,0:T(8,128)(2,1)S(1)} %collective-permute-done.5, bf16[22,192,3]{2,1,0:T(8,128)(2,1)S(1)} %bitcast.57, ...), kind=kLoop, calls=%fused_computation.1 | loop fusion | flops 12976128 | bytes 3295232 | tf_op jit(solution)/shard_map/concatenate | solution.py:47
  147.9 17.5 %shard_map.120 = bf16[16,192,128]{2,1,0:T(8,128)(2,1)} custom-call(bf16[22,192,256]{2,1,0:T(8,128)(2,1)} %maximum_maximum_fusion.1.ext_ref, bf16[16,192,128]{2,1,0:T(8,128)(2,1)} %bitcast.56, f32[4,1,512]{2,1,0:T(1,128)} %bitcast.75, f32[192,128]{1,0:T(8,128)} %pad.4.kernel_ref), custom_call_target="tpu_custom_call" | custom-call | flops 38535168 | bytes 6000000 | tf_op jit(solution)/shard_map/pallas_call | solution.py:411
  165.4 2.5 %copy.42 = bf16[192,16,128]{2,1,0:T(8,128)(2,1)} copy(bf16[192,16,128]{2,0,1:T(8,128)(2,1)} %bitcast.63) | data formatting | bytes 1572864
  (73 shorter events, 9.6 us)
Async XLA Ops:
  2.0 31.3 %copy-start.1 = (bf16[192,16,128]{2,0,1:T(8,128)(2,1)}, bf16[192,16,128]{2,0,1:T(8,128)(2,1)S(1)}, u32[]{:S(2)}) copy-start(bf16[192,16,128]{2,0,1:T(8,128)(2,1)S(1)} %copy.51) | copy-start | bytes 2359300
  2.0 7.0 %collective-permute-start.2 = (bf16[3,192,128]{2,1,0:T(8,128)(2,1)S(1)}, bf16[3,192,128]{2,1,0:T(8,128)(2,1)S(1)}, u32[]{:S(2)}, u32[]{:S(2)}) collective-permute-start(bf16[3,192,128]{2,1,0:T(8,128)(2,1)S(1)} %get-tuple-element.29), channel_id=1, source_target_pairs={{3,31},{7,27},{11,23},{15,19},{19,15},{23,11},{27,7},{31,3}} | collective-permute-start | bytes 442376 | tf_op jit(solution)/shard_map/ppermute | solution.py:28
  2.7 12.2 %collective-permute-start = (bf16[3,192,128]{2,1,0:T(8,128)(2,1)S(1)}, bf16[3,192,128]{2,1,0:T(8,128)(2,1)S(1)}, u32[]{:S(2)}, u32[]{:S(2)}) collective-permute-start(bf16[3,192,128]{2,1,0:T(8,128)(2,1)S(1)} %get-tuple-element.29), channel_id=1, source_target_pairs={{0,1},{1,2},{2,3},{4,5},{5,6},{6,7},{8,9},{9,10},{10,11},{12,13},{... | collective-permute-start | bytes 442376 | tf_op jit(solution)/shard_map/ppermute | solution.py:25
  7.6 7.2 %collective-permute-start.1 = (bf16[3,192,128]{2,1,0:T(8,128)(2,1)S(1)}, bf16[3,192,128]{2,1,0:T(8,128)(2,1)S(1)}, u32[]{:S(2)}, u32[]{:S(2)}) collective-permute-start(bf16[3,192,128]{2,1,0:T(8,128)(2,1)S(1)} %get-tuple-element.30), channel_id=1, source_target_pairs={{1,0},{2,1},{3,2},{5,4},{6,5},{7,6},{9,8},{10,9},{11,10},{13,12},{... | collective-permute-start | bytes 442376 | tf_op jit(solution)/shard_map/ppermute | solution.py:26
  9.0 5.9 %copy-start.7 = (bf16[128,128]{1,0:T(8,128)(2,1)}, bf16[128,128]{1,0:T(8,128)(2,1)S(1)}, u32[]{:S(2)}) copy-start(bf16[128,128]{1,0:T(8,128)(2,1)S(1)} %rev.11) | copy-start | bytes 98308
  15.5 7.9 %copy-start.9 = (s32[16,128]{1,0:T(8,128)S(1)}, s32[16,128]{1,0:T(8,128)}, u32[]{:S(2)}) copy-start(s32[16,128]{1,0:T(8,128)} %param.10) | copy-start | bytes 24580
  15.5 9.5 %copy-start.13 = (f32[192]{0:T(256)S(1)}, f32[192]{0:T(256)}, u32[]{:S(2)}) copy-start(f32[192]{0:T(256)} %param.15) | copy-start | bytes 2308
  15.6 10.2 %copy-start.10 = (f32[768]{0:T(1024)S(1)}, f32[768]{0:T(1024)}, u32[]{:S(2)}) copy-start(f32[768]{0:T(1024)} %param.13) | copy-start | bytes 9220
  15.6 11.1 %copy-start.3 = (bf16[192,768]{1,0:T(8,128)(2,1)S(1)}, bf16[192,768]{1,0:T(8,128)(2,1)}, u32[]{:S(2)}) copy-start(bf16[192,768]{1,0:T(8,128)(2,1)} %in_ref.1) | copy-start | bytes 884740
  16.7 10.9 %copy-start.4 = (bf16[768,192]{0,1:T(8,128)(2,1)S(1)}, bf16[768,192]{0,1:T(8,128)(2,1)}, u32[]{:S(2)}) copy-start(bf16[768,192]{0,1:T(8,128)(2,1)} %param.14) | copy-start | bytes 884740
  16.7 11.9 %copy-start.5 = (bf16[192,16,128]{2,1,0:T(8,128)(2,1)S(1)}, bf16[192,16,128]{2,1,0:T(8,128)(2,1)}, u32[]{:S(2)}) copy-start(bf16[192,16,128]{2,1,0:T(8,128)(2,1)} %param.9) | copy-start | bytes 2359300
  18.3 12.2 %collective-permute-start.3 = (bf16[66,192]{1,0:T(8,128)(2,1)}, bf16[66,192]{1,0:T(8,128)(2,1)}, u32[]{:S(2)}, u32[]{:S(2)}) collective-permute-start(bf16[66,192]{1,0:T(8,128)(2,1)} %reshape.65), channel_id=1, source_target_pairs={{0,4},{4,8},{8,12},{12,16},{16,20},{20,24},{24,28},{28,0},{1,5},{5... | collective-permute-start | bytes 76040 | tf_op jit(solution)/shard_map/ppermute | solution.py:42
  20.8 11.0 %collective-permute-start.4 = (bf16[66,192]{1,0:T(8,128)(2,1)}, bf16[66,192]{1,0:T(8,128)(2,1)}, u32[]{:S(2)}, u32[]{:S(2)}) collective-permute-start(bf16[66,192]{1,0:T(8,128)(2,1)} %reshape.67), channel_id=1, source_target_pairs={{4,0},{8,4},{12,8},{16,12},{20,16},{24,20},{28,24},{0,28},{5,1},{9... | collective-permute-start | bytes 76040 | tf_op jit(solution)/shard_map/ppermute | solution.py:45
  29.8 6.6 %copy-start.11 = (bf16[256]{0:T(256)(128)(2,1)}, bf16[256]{0:T(256)(128)(2,1)S(1)}, u32[]{:S(2)}) copy-start(bf16[256]{0:T(256)(128)(2,1)S(1)} %pad.19.clone) | copy-start | bytes 1540
  71.6 62.0 %collective-permute-start.7 = (bf16[3,192,128]{2,1,0:T(8,128)(2,1)S(1)}, bf16[3,192,128]{2,1,0:T(8,128)(2,1)S(1)}, u32[]{:S(2)}, u32[]{:S(2)}) collective-permute-start(bf16[3,192,128]{2,1,0:T(8,128)(2,1)S(1)} %get-tuple-element.27), channel_id=1, source_target_pairs={{3,31},{7,27},{11,23},{15,19},{19,15},{23,11},{27,7},{31,3}} | collective-permute-start | bytes 442376 | tf_op jit(solution)/shard_map/ppermute | solution.py:28
  72.3 61.6 %collective-permute-start.5 = (bf16[3,192,128]{2,1,0:T(8,128)(2,1)S(1)}, bf16[3,192,128]{2,1,0:T(8,128)(2,1)S(1)}, u32[]{:S(2)}, u32[]{:S(2)}) collective-permute-start(bf16[3,192,128]{2,1,0:T(8,128)(2,1)S(1)} %get-tuple-element.27), channel_id=1, source_target_pairs={{0,1},{1,2},{2,3},{4,5},{5,6},{6,7},{8,9},{9,10},{10,11},{12,13},{... | collective-permute-start | bytes 442376 | tf_op jit(solution)/shard_map/ppermute | solution.py:25
  73.6 60.3 %collective-permute-start.6 = (bf16[3,192,128]{2,1,0:T(8,128)(2,1)S(1)}, bf16[3,192,128]{2,1,0:T(8,128)(2,1)S(1)}, u32[]{:S(2)}, u32[]{:S(2)}) collective-permute-start(bf16[3,192,128]{2,1,0:T(8,128)(2,1)S(1)} %get-tuple-element.28), channel_id=1, source_target_pairs={{1,0},{2,1},{3,2},{5,4},{6,5},{7,6},{9,8},{10,9},{11,10},{13,12},{... | collective-permute-start | bytes 442376 | tf_op jit(solution)/shard_map/ppermute | solution.py:26
  75.1 1.3 copy-start
  131.1 2.6 %copy-start.8 = (bf16[128,128]{1,0:T(8,128)(2,1)S(1)}, bf16[128,128]{1,0:T(8,128)(2,1)}, u32[]{:S(2)}) copy-start(bf16[128,128]{1,0:T(8,128)(2,1)} %copy-done.7) | copy-start | bytes 98308
  131.2 2.8 %copy-start.2 = (bf16[16,192,128]{2,1,0:T(8,128)(2,1)S(1)}, bf16[16,192,128]{2,1,0:T(8,128)(2,1)}, u32[]{:S(2)}) copy-start(bf16[16,192,128]{2,1,0:T(8,128)(2,1)} %get-tuple-element.9) | copy-start | bytes 2359300
  138.0 6.2 %collective-permute-start.9 = (bf16[66,192]{1,0:T(8,128)(2,1)S(1)}, bf16[66,192]{1,0:T(8,128)(2,1)S(1)}, u32[]{:S(2)}, u32[]{:S(2)}) collective-permute-start(bf16[66,192]{1,0:T(8,128)(2,1)S(1)} %reshape.75), channel_id=1, source_target_pairs={{4,0},{8,4},{12,8},{16,12},{20,16},{24,20},{28,24},{0,28},{5,1},{9... | collective-permute-start | bytes 76040 | tf_op jit(solution)/shard_map/ppermute | solution.py:45
  138.0 5.4 %collective-permute-start.8 = (bf16[66,192]{1,0:T(8,128)(2,1)S(1)}, bf16[66,192]{1,0:T(8,128)(2,1)S(1)}, u32[]{:S(2)}, u32[]{:S(2)}) collective-permute-start(bf16[66,192]{1,0:T(8,128)(2,1)S(1)} %reshape.73), channel_id=1, source_target_pairs={{0,4},{4,8},{8,12},{12,16},{16,20},{20,24},{24,28},{28,0},{1,5},{5... | collective-permute-start | bytes 76040 | tf_op jit(solution)/shard_map/ppermute | solution.py:42
  138.5 2.8 %copy-start.6 = (bf16[16,192,128]{2,1,0:T(8,128)(2,1)S(1)}, bf16[16,192,128]{2,1,0:T(8,128)(2,1)}, u32[]{:S(2)}) copy-start(bf16[16,192,128]{2,1,0:T(8,128)(2,1)} %get-tuple-element.8) | copy-start | bytes 2359300
  141.3 3.5 %copy-start.12 = (bf16[256]{0:T(256)(128)(2,1)S(1)}, bf16[256]{0:T(256)(128)(2,1)}, u32[]{:S(2)}) copy-start(bf16[256]{0:T(256)(128)(2,1)} %copy-done.11) | copy-start | bytes 1540

commit v3 on v2

--- a/solution.py
+++ b/solution.py
@@ -246,7 +246,8 @@
 def sum_kernel(route, factor, part_ref, result_ref, held_ref, final_ref, *rest):
     count = len(route)
     inbox = rest[:count]
-    send_sem, recv_sem, back_send_sem, back_recv_sem = rest[count:]
+    outbox = rest[count : 2 * count]
+    send_sem, recv_sem, back_send_sem, back_recv_sem = rest[2 * count :]
     partners = []
     for axis, bit in route:
         me = lax.axis_index(axis)
@@ -266,8 +267,9 @@
         size = size // 2
         keep = pl.ds(pl.multiple_of(base + mine * size, 16), size)
         give = pl.ds(pl.multiple_of(base + (1 - mine) * size, 16), size)
+        outbox[k][...] = source[give, :].astype(BF16)
         copy = pltpu.make_async_remote_copy(
-            src_ref=source.at[give],
+            src_ref=outbox[k],
             dst_ref=inbox[k],
             send_sem=send_sem.at[k],
             recv_sem=recv_sem.at[k],
@@ -276,7 +278,7 @@
         )
         copy.start()
         copy.wait()
-        held_ref[keep, :] = source[keep, :] + inbox[k][...]
+        held_ref[keep, :] = source[keep, :] + inbox[k][...].astype(F32)
         source = held_ref
         base = base + mine * size
     own = pl.ds(pl.multiple_of(base, 16), size)
@@ -312,7 +314,7 @@
         out_specs=pl.BlockSpec(memory_space=pltpu.VMEM),
         out_shape=jax.ShapeDtypeStruct(part.shape, F32),
         scratch_shapes=[pltpu.VMEM(part.shape, F32), pltpu.VMEM(part.shape, BF16)]
-        + [pltpu.VMEM((rows >> (k + 1), LANES), F32) for k in range(count)]
+        + 2 * [pltpu.VMEM((rows >> (k + 1), LANES), BF16) for k in range(count)]
         + [pltpu.SemaphoreType.DMA((count,))] * 4,
         compiler_params=pltpu.CompilerParams(
             collective_id=0, has_side_effects=True, vmem_limit_bytes=24 * 1024 * 1024

time: 169 us -> 163 us (0.964)
  Pallas kernels: 106 us -> 99.2 us
    pallas_call x1, Pallas kernels: 54.7 us -> 41.9 us  [sum_devices(): pl.pallas_call(functools.partial(sum_kernel, tuple(route), factor), in_sp...]
    pallas_call x1, Pallas kernels: 34.2 us -> 39.8 us  [per_device(): pl.pallas_call(main_kernel, grid=(steps,), in_specs=[whole(ext_shape), bl...]
  transfers between devices with their start and end apart: 10 -> 10, of which waited for: 1 -> 1; matrix products, arithmetic and copies ran while one was open for 12% -> 12% of each run, Pallas kernels for 33% -> 26%
where the time goes in v3:
time: 163 us; the launch traced here: 161 us
  Pallas kernels  99.2 us (61%)
  local copies, waits for them, and re-layouts  33.9 us (21%)
  starting transfers between devices  13.9 us (9%)
  other arithmetic  7.09 us (4%)
  waiting for transfers between devices  5.66 us (3%)
    pallas_call x1, Pallas kernels, sum_devices(): pl.pallas_call(functools.partial(sum_kernel, tuple(route), factor), in_sp...  41.9 us
    pallas_call x1, Pallas kernels, per_device(): pl.pallas_call(main_kernel, grid=(steps,), in_specs=[whole(ext_shape), bl...  39.8 us
    pallas_call x1, Pallas kernels, per_device(): pl.pallas_call(field_kernel, grid=(steps,), in_specs=[whole(ext_shape), b...  17.5 us
    unnamed x35, local copies, waits for them, and re-layouts  9.7 us
    ppermute x2, starting transfers between devices, extend(): south = lax.ppermute(top, 'gy', [(i, i + 1) for i in range(ny - 1)])  6.62 us
    transpose x6, local copies, waits for them, and re-layouts, pack(): return jnp.transpose(part, (0, 2, 1)).reshape((height + 6) * 3, channels)  6.51 us
    concatenate x2, other arithmetic, extend(): return jnp.concatenate([unpack(left), tall, unpack(right), spare], axis=2)  6.13 us
    ppermute x2, waiting for transfers between devices, extend(): north = lax.ppermute(bottom, 'gy', [(i + 1, i) for i in range(ny - 1)])  5.64 us
  transfers between devices with their start and end apart: 10, of which 1 were waited for; matrix products, arithmetic and copies ran while one was open for 12% of the time, Pallas kernels for 26%

profile of v3, /device:TPU:0, one launch (start us, length us, event | category | flops | bytes accessed | tf_op | source)
XLA Modules:
  0.0 161.2 jit_solution(3279396859067690182)
XLA Ops:
  0.6 1.3 copy.51
  2.7 4.9 %collective-permute-start = (bf16[3,192,128]{2,1,0:T(8,128)(2,1)S(1)}, bf16[3,192,128]{2,1,0:T(8,128)(2,1)S(1)}, u32[]{:S(2)}, u32[]{:S(2)}) collective-permute-start(bf16[3,192,128]{2,1,0:T(8,128)(2,1)S(1)} %get-tuple-element.29), channel_id=1, source_target_pairs={{0,1},{1,2},{2,3},{4,5},{5,6},{6,7},{8,9},{9,10},{10,11},{12,13},{... | collective-permute-start | bytes 442376 | tf_op jit(solution)/shard_map/ppermute | solution.py:25
  7.6 1.3 collective-permute-start.1
  9.2 5.6 %collective-permute-done.1 = bf16[3,192,128]{2,1,0:T(8,128)(2,1)S(1)} collective-permute-done((bf16[3,192,128]{2,1,0:T(8,128)(2,1)S(1)}, bf16[3,192,128]{2,1,0:T(8,128)(2,1)S(1)}, u32[]{:S(2)}, u32[]{:S(2)}) %collective-permute-start.1) | collective-permute-done | bytes 147488 | tf_op jit(solution)/shard_map/ppermute | solution.py:26
  15.6 1.1 copy.24
  16.7 1.5 reshape.65
  18.3 1.1 copy.26
  19.4 1.4 reshape.67
  20.8 2.6 %collective-permute-start.4 = (bf16[66,192]{1,0:T(8,128)(2,1)}, bf16[66,192]{1,0:T(8,128)(2,1)}, u32[]{:S(2)}, u32[]{:S(2)}) collective-permute-start(bf16[66,192]{1,0:T(8,128)(2,1)} %reshape.67), channel_id=1, source_target_pairs={{4,0},{8,4},{12,8},{16,12},{20,16},{24,20},{28,24},{0,28},{5,1},{9... | collective-permute-start | bytes 76040 | tf_op jit(solution)/shard_map/ppermute | solution.py:45
  24.1 0.8 reshape.70
  25.8 0.9 broadcast_in_dim.8.bias_ref
  26.7 0.9 copy.30
  27.6 1.0 copy.32.out_ref
  28.6 1.1 copy.50
  30.4 0.8 reshape.66
  31.9 0.8 reshape.68
  33.3 3.1 %maximum_maximum_fusion.ext_ref = bf16[22,192,256]{2,1,0:T(8,128)(2,1)} fusion(bf16[22,192,3]{2,1,0:T(8,128)(2,1)S(1)} %bitcast.60, bf16[3,192,128]{2,1,0:T(8,128)(2,1)S(1)} %add.8, bf16[16,192,128]{2,1,0:T(8,128)(2,1)S(1)} %bitcast.53, bf16[3,192,128]{2,1,0:T(8,128)(2,1)S(1)} %collective-permute-done, bf16[22,192,3]{2,1,0:T(8,128)(2,1)S(1)} %bitcast.58, ...), kind=kLoop, calls=%fused_computation | loop fusion | flops 12976128 | bytes 3295232 | tf_op jit(solution)/shard_map/concatenate | solution.py:47
  36.4 39.8 %shard_map.119 = (bf16[16,192,128]{2,1,0:T(8,128)(2,1)}, bf16[16,192,128]{2,1,0:T(8,128)(2,1)}, f32[2560,128]{1,0:T(8,128)}) custom-call(bf16[22,192,256]{2,1,0:T(8,128)(2,1)} %maximum_maximum_fusion.ext_ref, bf16[16,192,128]{2,1,0:T(8,128)(2,1)} %bitcast.54, bf16[16,192,128]{2,1,0:T(8,128)(2,1)} %bitcast.55, f32[4,1,512]{2,1,0:T(1,128)} %bitcast.74, ...), custom_call_target="tpu_custom_call" | custom-call | tf_op jit(solution)/shard_map/pallas_call | solution.py:362
  76.2 1.0 fusion.2
  77.9 1.7 %collective-permute-start.5 = (bf16[3,192,128]{2,1,0:T(8,128)(2,1)S(1)}, bf16[3,192,128]{2,1,0:T(8,128)(2,1)S(1)}, u32[]{:S(2)}, u32[]{:S(2)}) collective-permute-start(bf16[3,192,128]{2,1,0:T(8,128)(2,1)S(1)} %get-tuple-element.27), channel_id=1, source_target_pairs={{0,1},{1,2},{2,3},{4,5},{5,6},{6,7},{8,9},{9,10},{10,11},{12,13},{... | collective-permute-start | bytes 442376 | tf_op jit(solution)/shard_map/ppermute | solution.py:25
  79.6 1.5 collective-permute-start.6
  81.1 1.3 copy-done
  82.4 41.9 %shard_map.121 = f32[2560,128]{1,0:T(8,128)S(1)} custom-call(f32[2560,128]{1,0:T(8,128)S(1)} %copy-done), custom_call_target="tpu_custom_call" | custom-call | tf_op jit(solution)/shard_map/pallas_call | solution.py:311
  124.4 1.3 copy.39
  125.7 1.2 copy.40
  127.3 1.5 slice_bitcast_fusion.1
  128.8 1.7 %copy.34 = bf16[22,3,192]{2,1,0:T(4,128)(2,1)S(1)} copy(bf16[22,3,192]{1,2,0:T(8,128)(2,1)} %get-tuple-element.23) | data formatting | bytes 50688 | tf_op jit(solution)/shard_map/transpose | solution.py:37
  131.8 2.7 %copy_bitcast_fusion.2 = (f32[768,192]{0,1:T(8,128)}, f32[192,768]{1,0:T(8,128)}) fusion(f32[24,8,6,128]{3,2,1,0:T(8,128)} %bitcast.62, f32[24,8,6,128]{3,2,1,0:T(8,128)} %bitcast.61), kind=kLoop, calls=%fused_computation.12 | loop fusion | bytes 2359296 | tf_op jit(solution)/shard_map/reshape | solution.py:410
  134.6 1.4 copy.41
  138.1 3.1 %maximum_maximum_fusion.1.ext_ref = bf16[22,192,256]{2,1,0:T(8,128)(2,1)} fusion(bf16[22,192,3]{2,1,0:T(8,128)(2,1)S(1)} %bitcast.59, bf16[3,192,128]{2,1,0:T(8,128)(2,1)S(1)} %add.9, bf16[16,192,128]{2,1,0:T(8,128)(2,1)S(1)} %copy-done.2, bf16[3,192,128]{2,1,0:T(8,128)(2,1)S(1)} %collective-permute-done.5, bf16[22,192,3]{2,1,0:T(8,128)(2,1)S(1)} %bitcast.57, ...), kind=kLoop, calls=%fused_computation.1 | loop fusion | flops 12976128 | bytes 3295232 | tf_op jit(solution)/shard_map/concatenate | solution.py:47
  141.1 17.5 %shard_map.120 = bf16[16,192,128]{2,1,0:T(8,128)(2,1)} custom-call(bf16[22,192,256]{2,1,0:T(8,128)(2,1)} %maximum_maximum_fusion.1.ext_ref, bf16[16,192,128]{2,1,0:T(8,128)(2,1)} %bitcast.56, f32[4,1,512]{2,1,0:T(1,128)} %bitcast.75, f32[192,128]{1,0:T(8,128)} %pad.4.kernel_ref), custom_call_target="tpu_custom_call" | custom-call | flops 38535168 | bytes 6000000 | tf_op jit(solution)/shard_map/pallas_call | solution.py:413
  158.6 2.5 %copy.42 = bf16[192,16,128]{2,1,0:T(8,128)(2,1)} copy(bf16[192,16,128]{2,0,1:T(8,128)(2,1)} %bitcast.63) | data formatting | bytes 1572864
  (73 shorter events, 9.6 us)
Async XLA Ops:
  2.0 31.3 %copy-start.1 = (bf16[192,16,128]{2,0,1:T(8,128)(2,1)}, bf16[192,16,128]{2,0,1:T(8,128)(2,1)S(1)}, u32[]{:S(2)}) copy-start(bf16[192,16,128]{2,0,1:T(8,128)(2,1)S(1)} %copy.51) | copy-start | bytes 2359300
  2.0 7.0 %collective-permute-start.2 = (bf16[3,192,128]{2,1,0:T(8,128)(2,1)S(1)}, bf16[3,192,128]{2,1,0:T(8,128)(2,1)S(1)}, u32[]{:S(2)}, u32[]{:S(2)}) collective-permute-start(bf16[3,192,128]{2,1,0:T(8,128)(2,1)S(1)} %get-tuple-element.29), channel_id=1, source_target_pairs={{3,31},{7,27},{11,23},{15,19},{19,15},{23,11},{27,7},{31,3}} | collective-permute-start | bytes 442376 | tf_op jit(solution)/shard_map/ppermute | solution.py:28
  2.7 12.2 %collective-permute-start = (bf16[3,192,128]{2,1,0:T(8,128)(2,1)S(1)}, bf16[3,192,128]{2,1,0:T(8,128)(2,1)S(1)}, u32[]{:S(2)}, u32[]{:S(2)}) collective-permute-start(bf16[3,192,128]{2,1,0:T(8,128)(2,1)S(1)} %get-tuple-element.29), channel_id=1, source_target_pairs={{0,1},{1,2},{2,3},{4,5},{5,6},{6,7},{8,9},{9,10},{10,11},{12,13},{... | collective-permute-start | bytes 442376 | tf_op jit(solution)/shard_map/ppermute | solution.py:25
  7.6 7.2 %collective-permute-start.1 = (bf16[3,192,128]{2,1,0:T(8,128)(2,1)S(1)}, bf16[3,192,128]{2,1,0:T(8,128)(2,1)S(1)}, u32[]{:S(2)}, u32[]{:S(2)}) collective-permute-start(bf16[3,192,128]{2,1,0:T(8,128)(2,1)S(1)} %get-tuple-element.30), channel_id=1, source_target_pairs={{1,0},{2,1},{3,2},{5,4},{6,5},{7,6},{9,8},{10,9},{11,10},{13,12},{... | collective-permute-start | bytes 442376 | tf_op jit(solution)/shard_map/ppermute | solution.py:26
  9.0 5.9 %copy-start.7 = (bf16[128,128]{1,0:T(8,128)(2,1)}, bf16[128,128]{1,0:T(8,128)(2,1)S(1)}, u32[]{:S(2)}) copy-start(bf16[128,128]{1,0:T(8,128)(2,1)S(1)} %rev.11) | copy-start | bytes 98308
  15.5 7.9 %copy-start.9 = (s32[16,128]{1,0:T(8,128)S(1)}, s32[16,128]{1,0:T(8,128)}, u32[]{:S(2)}) copy-start(s32[16,128]{1,0:T(8,128)} %param.10) | copy-start | bytes 24580
  15.5 9.5 %copy-start.13 = (f32[192]{0:T(256)S(1)}, f32[192]{0:T(256)}, u32[]{:S(2)}) copy-start(f32[192]{0:T(256)} %param.15) | copy-start | bytes 2308
  15.6 10.2 %copy-start.10 = (f32[768]{0:T(1024)S(1)}, f32[768]{0:T(1024)}, u32[]{:S(2)}) copy-start(f32[768]{0:T(1024)} %param.13) | copy-start | bytes 9220
  15.6 11.1 %copy-start.3 = (bf16[192,768]{1,0:T(8,128)(2,1)S(1)}, bf16[192,768]{1,0:T(8,128)(2,1)}, u32[]{:S(2)}) copy-start(bf16[192,768]{1,0:T(8,128)(2,1)} %in_ref.1) | copy-start | bytes 884740
  16.7 10.9 %copy-start.4 = (bf16[768,192]{0,1:T(8,128)(2,1)S(1)}, bf16[768,192]{0,1:T(8,128)(2,1)}, u32[]{:S(2)}) copy-start(bf16[768,192]{0,1:T(8,128)(2,1)} %param.14) | copy-start | bytes 884740
  16.7 11.9 %copy-start.5 = (bf16[192,16,128]{2,1,0:T(8,128)(2,1)S(1)}, bf16[192,16,128]{2,1,0:T(8,128)(2,1)}, u32[]{:S(2)}) copy-start(bf16[192,16,128]{2,1,0:T(8,128)(2,1)} %param.9) | copy-start | bytes 2359300
  18.3 12.2 %collective-permute-start.3 = (bf16[66,192]{1,0:T(8,128)(2,1)}, bf16[66,192]{1,0:T(8,128)(2,1)}, u32[]{:S(2)}, u32[]{:S(2)}) collective-permute-start(bf16[66,192]{1,0:T(8,128)(2,1)} %reshape.65), channel_id=1, source_target_pairs={{0,4},{4,8},{8,12},{12,16},{16,20},{20,24},{24,28},{28,0},{1,5},{5... | collective-permute-start | bytes 76040 | tf_op jit(solution)/shard_map/ppermute | solution.py:42
  20.8 11.0 %collective-permute-start.4 = (bf16[66,192]{1,0:T(8,128)(2,1)}, bf16[66,192]{1,0:T(8,128)(2,1)}, u32[]{:S(2)}, u32[]{:S(2)}) collective-permute-start(bf16[66,192]{1,0:T(8,128)(2,1)} %reshape.67), channel_id=1, source_target_pairs={{4,0},{8,4},{12,8},{16,12},{20,16},{24,20},{28,24},{0,28},{5,1},{9... | collective-permute-start | bytes 76040 | tf_op jit(solution)/shard_map/ppermute | solution.py:45
  29.8 6.6 %copy-start.11 = (bf16[256]{0:T(256)(128)(2,1)}, bf16[256]{0:T(256)(128)(2,1)S(1)}, u32[]{:S(2)}) copy-start(bf16[256]{0:T(256)(128)(2,1)S(1)} %pad.19.clone) | copy-start | bytes 1540
  77.2 49.7 %collective-permute-start.7 = (bf16[3,192,128]{2,1,0:T(8,128)(2,1)S(1)}, bf16[3,192,128]{2,1,0:T(8,128)(2,1)S(1)}, u32[]{:S(2)}, u32[]{:S(2)}) collective-permute-start(bf16[3,192,128]{2,1,0:T(8,128)(2,1)S(1)} %get-tuple-element.27), channel_id=1, source_target_pairs={{3,31},{7,27},{11,23},{15,19},{19,15},{23,11},{27,7},{31,3}} | collective-permute-start | bytes 442376 | tf_op jit(solution)/shard_map/ppermute | solution.py:28
  77.9 49.3 %collective-permute-start.5 = (bf16[3,192,128]{2,1,0:T(8,128)(2,1)S(1)}, bf16[3,192,128]{2,1,0:T(8,128)(2,1)S(1)}, u32[]{:S(2)}, u32[]{:S(2)}) collective-permute-start(bf16[3,192,128]{2,1,0:T(8,128)(2,1)S(1)} %get-tuple-element.27), channel_id=1, source_target_pairs={{0,1},{1,2},{2,3},{4,5},{5,6},{6,7},{8,9},{9,10},{10,11},{12,13},{... | collective-permute-start | bytes 442376 | tf_op jit(solution)/shard_map/ppermute | solution.py:25
  79.6 47.5 %collective-permute-start.6 = (bf16[3,192,128]{2,1,0:T(8,128)(2,1)S(1)}, bf16[3,192,128]{2,1,0:T(8,128)(2,1)S(1)}, u32[]{:S(2)}, u32[]{:S(2)}) collective-permute-start(bf16[3,192,128]{2,1,0:T(8,128)(2,1)S(1)} %get-tuple-element.28), channel_id=1, source_target_pairs={{1,0},{2,1},{3,2},{5,4},{6,5},{7,6},{9,8},{10,9},{11,10},{13,12},{... | collective-permute-start | bytes 442376 | tf_op jit(solution)/shard_map/ppermute | solution.py:26
  81.1 1.3 copy-start
  124.3 2.6 %copy-start.8 = (bf16[128,128]{1,0:T(8,128)(2,1)S(1)}, bf16[128,128]{1,0:T(8,128)(2,1)}, u32[]{:S(2)}) copy-start(bf16[128,128]{1,0:T(8,128)(2,1)} %copy-done.7) | copy-start | bytes 98308
  124.4 2.8 %copy-start.2 = (bf16[16,192,128]{2,1,0:T(8,128)(2,1)S(1)}, bf16[16,192,128]{2,1,0:T(8,128)(2,1)}, u32[]{:S(2)}) copy-start(bf16[16,192,128]{2,1,0:T(8,128)(2,1)} %get-tuple-element.9) | copy-start | bytes 2359300
  131.2 6.2 %collective-permute-start.9 = (bf16[66,192]{1,0:T(8,128)(2,1)S(1)}, bf16[66,192]{1,0:T(8,128)(2,1)S(1)}, u32[]{:S(2)}, u32[]{:S(2)}) collective-permute-start(bf16[66,192]{1,0:T(8,128)(2,1)S(1)} %reshape.75), channel_id=1, source_target_pairs={{4,0},{8,4},{12,8},{16,12},{20,16},{24,20},{28,24},{0,28},{5,1},{9... | collective-permute-start | bytes 76040 | tf_op jit(solution)/shard_map/ppermute | solution.py:45
  131.3 5.4 %collective-permute-start.8 = (bf16[66,192]{1,0:T(8,128)(2,1)S(1)}, bf16[66,192]{1,0:T(8,128)(2,1)S(1)}, u32[]{:S(2)}, u32[]{:S(2)}) collective-permute-start(bf16[66,192]{1,0:T(8,128)(2,1)S(1)} %reshape.73), channel_id=1, source_target_pairs={{0,4},{4,8},{8,12},{12,16},{16,20},{20,24},{24,28},{28,0},{1,5},{5... | collective-permute-start | bytes 76040 | tf_op jit(solution)/shard_map/ppermute | solution.py:42
  131.8 2.8 %copy-start.6 = (bf16[16,192,128]{2,1,0:T(8,128)(2,1)S(1)}, bf16[16,192,128]{2,1,0:T(8,128)(2,1)}, u32[]{:S(2)}) copy-start(bf16[16,192,128]{2,1,0:T(8,128)(2,1)} %get-tuple-element.8) | copy-start | bytes 2359300
  134.6 3.5 %copy-start.12 = (bf16[256]{0:T(256)(128)(2,1)S(1)}, bf16[256]{0:T(256)(128)(2,1)}, u32[]{:S(2)}) copy-start(bf16[256]{0:T(256)(128)(2,1)} %copy-done.11) | copy-start | bytes 1540
